TPU v7x, 512 devices: a whole 4x8x8 slice. The times are simulated.
512 devices in a mesh: px: 32 (over x_hi, y, core), py: 16 (over x_lo, z).
Axes of the slice: x: 4 (x_hi: 2, x_lo: 2; x = x_hi * 2 + x_lo), y: 8, z: 8, core: 2. Of those that a mesh axis runs over, the one named last changes fastest.
Arguments:
- trial_block: float32 [32, 16, 2, 8, 8192], P('px', 'py'), may hold values from -12 to 12
- stiff_coef: float32 [32, 16, 1024], P('px', 'py'), may hold values from 0.3 to 3
- mass_coef: float32 [32, 16, 1024], P('px', 'py'), may hold values from 1 to 12
- elem_count: int32 [32, 16], P('px', 'py'), may hold values from 256 to 1024, as said below
- elem_dofs: int32 [32, 16, 1024, 20], P('px', 'py'), may hold values from 0 to 12287, as said below
- pairing: int32 [2048], replicated, may hold values from 0 to 2047, each once
- bloch_fraction: int32 [2], replicated, may hold values from 1 to 16, as said below
- stiff_ref: float32 [20, 20], replicated, may hold values from -16 to 17, as said below
- mass_ref: float32 [20, 20], replicated, may hold values from -16 to 17, as said below
Outputs:
- curl_image: float32 [32, 16, 2, 8, 8192], P('px', 'py')
- mass_image: float32 [32, 16, 2, 8, 8192], P('px', 'py')
- gram: float32 [2, 2, 8, 8], replicated
Inputs may be any that keep to these rules, and one draw needn't show every extreme that they name: `elem_count`: element slots below 128 are the only ones that name indices of 8192 or more; each part's count is at least 256, and each part of a 2-by-2 block of parts has exactly 1024 in every draw. `elem_dofs`: indices into the extended layout; slots at or above 128 name only indices below 8192. bloch_fraction[1] is 16 and 0 < bloch_fraction[0] < bloch_fraction[1]. `stiff_ref`: symmetric positive definite. `mass_ref`: symmetric positive definite.
All inputs are finite; a program needn't handle non-finite values.
Results may differ from a plain program's by a relative error of at most 0.0003.
Values sent between devices are 32-bit elements; how exact they have to be, the bound alone decides.
A program may use at most 64 MiB of HBM per device.

v0:
```python
import functools
import math

import jax
import jax.numpy as jnp
from jax import lax
from jax.experimental import pallas as pl
from jax.experimental.pallas import tpu as pltpu
from jax.sharding import PartitionSpec as P

HIGH = lax.Precision.HIGHEST
LANES = 128
ROWS = 16
NLOC = 20
HALO_SLOTS = 128
BLOCK = 128
TILES = 5
GTILES = 3
LANE_SETS = 4

VMEM = pl.BlockSpec(memory_space=pltpu.VMEM)
SMEM = pl.BlockSpec(memory_space=pltpu.SMEM)


def split_bf16(value):
    high = value.astype(jnp.bfloat16)
    low = (value - high.astype(jnp.float32)).astype(jnp.bfloat16)
    return high, low


def dot_split(a, b):
    (ah, al), (bh, bl) = a, b
    dot = functools.partial(jnp.dot, preferred_element_type=jnp.float32)
    return dot(ah, bh) + (dot(al, bh) + dot(ah, bl))


def prepare_kernel(wrap_ref, dofs_ref, pairing_ref, stiff_ref, mass_ref, idx_out, kh_out, kl_out):
    face = pairing_ref.shape[0] * LANES
    owned = 4 * face
    idx_out[...] = dofs_ref[...]
    head = dofs_ref[:, :HALO_SLOTS]
    spot = head - owned
    local = spot & (LANES - 1)
    found = jnp.zeros_like(head)
    for row in range(pairing_ref.shape[0]):
        values = jnp.broadcast_to(pairing_ref[row : row + 1, :], head.shape)
        here = jnp.take_along_axis(values, local, axis=1)
        found = jnp.where((spot >> 7) == row, here + owned, found)
    wraps = (spot >= 0) & (spot < face) & (wrap_ref[0] == 1)
    idx_out[:, :HALO_SLOTS] = jnp.where(wraps, found, head)

    grow = lax.broadcasted_iota(jnp.int32, (GTILES * LANES, NLOC), 0)
    gcol = lax.broadcasted_iota(jnp.int32, (GTILES * LANES, NLOC), 1)
    spread_i = ((grow >> 4) == gcol).astype(jnp.float32)
    trow = lax.broadcasted_iota(jnp.int32, (NLOC, TILES * LANES), 0)
    tcol = lax.broadcasted_iota(jnp.int32, (NLOC, TILES * LANES), 1)
    spread_j = ((tcol >> 5) == trow).astype(jnp.float32)
    dot = functools.partial(jnp.dot, precision=HIGH, preferred_element_type=jnp.float32)
    stiff = dot(dot(spread_i, stiff_ref[...].T), spread_j)
    mass = dot(dot(spread_i, mass_ref[...].T), spread_j)
    krow = lax.broadcasted_iota(jnp.int32, (GTILES * LANES, TILES * LANES), 0)
    kcol = lax.broadcasted_iota(jnp.int32, (GTILES * LANES, TILES * LANES), 1)
    both = jnp.where(((kcol >> 4) & 1) == 0, stiff, mass)
    both = jnp.where((krow & 15) == (kcol & 15), both, 0.0)
    kh_out[...], kl_out[...] = split_bf16(both)


def part_kernel(
    count_ref,
    phase_ref,
    idx_s,
    idx_v,
    own_ref,
    high_x_ref,
    high_y_ref,
    stiff_ref,
    mass_ref,
    kh_ref,
    kl_ref,
    curl_out,
    mass_out,
    side_x_out,
    side_y_out,
    gram_out,
    ext,
    acc0,
    acc1,
    acc2,
    acc3,
    gathered,
    terms,
    gram,
):
    accs = (acc0, acc1, acc2, acc3)
    owned = own_ref.shape[1]
    face = high_x_ref.shape[1]
    cosine, sine = phase_ref[0], phase_ref[1]
    count = count_ref[0, 0]

    def put_rows(at, block):
        ext[pl.ds(at, LANES), :] = jnp.concatenate([block] * (LANES // ROWS), axis=0).T

    @pl.loop(0, owned // LANES)
    def _(b):
        at = pl.multiple_of(b * LANES, LANES)
        put_rows(at, own_ref[:, pl.ds(at, LANES)])

    @pl.loop(0, face // LANES)
    def _(b):
        at = pl.multiple_of(b * LANES, LANES)
        got = high_x_ref[:, pl.ds(at, LANES)]
        real, imag = got[: ROWS // 2], got[ROWS // 2 :]
        turned = jnp.concatenate([cosine * real - sine * imag, sine * real + cosine * imag], axis=0)
        put_rows(owned + at, turned)
        put_rows(owned + face + at, high_y_ref[:, pl.ds(at, LANES)])

    zero_rows = jnp.zeros((LANES, LANES), jnp.float32)

    @pl.loop(0, ext.shape[0] // LANES)
    def _(b):
        at = pl.multiple_of(b * LANES, LANES)
        for acc in accs:
            acc[pl.ds(at, LANES), :] = zero_rows

    gram[...] = jnp.zeros_like(gram)
    lane_set = lax.broadcasted_iota(jnp.int32, (1, LANES), 1) >> 4

    @pl.loop(0, (count + BLOCK - 1) // BLOCK)
    def _(block_id):
        first = pl.multiple_of(block_id * BLOCK, BLOCK)

        @pl.loop(0, BLOCK, unroll=4)
        def _(e):
            slot = first + e
            for tile in range(GTILES):
                inside = range(8 * tile, min(8 * tile + 8, NLOC))
                row = None
                for i in inside:
                    got = ext[pl.ds(idx_s[i, slot], 1), :]
                    row = got if row is None else jnp.where(lane_set == i % 8, got, row)
                gathered[tile, pl.ds(e, 1), :] = row

        values = jnp.concatenate([gathered[tile] for tile in range(GTILES)], axis=1)
        pieces = split_bf16(values)
        products = dot_split(pieces, (kh_ref[...], kl_ref[...]))
        slots = first + lax.broadcasted_iota(jnp.int32, (1, BLOCK), 1)
        live = slots < count
        stiff = jnp.where(live, stiff_ref[:, pl.ds(first, BLOCK)], 0.0)
        mass = jnp.where(live, mass_ref[:, pl.ds(first, BLOCK)], 0.0)
        pair = [jnp.broadcast_to(stiff, (ROWS, BLOCK)), jnp.broadcast_to(mass, (ROWS, BLOCK))]
        coef = jnp.concatenate(pair * LANE_SETS, axis=0).T
        scaled = [products[:, t * LANES : (t + 1) * LANES] * coef for t in range(TILES)]

        turned = split_bf16(values.T)
        for t in range(TILES):
            gram[:, t * LANES : (t + 1) * LANES] += dot_split(turned, split_bf16(scaled[t]))

        names = []
        for t in range(TILES):
            rows = [
                jnp.broadcast_to(idx_v[j : j + 1, pl.ds(first, BLOCK)], (LANES // LANE_SETS, BLOCK))
                for j in range(LANE_SETS * t, LANE_SETS * t + LANE_SETS)
            ]
            names.append(jnp.concatenate(rows, axis=0).astype(jnp.float32).T)
        for t in range(TILES):
            total = scaled[t]
            for s in range(t):
                total = total + jnp.where(names[s] == names[t], scaled[s], 0.0)
            terms[t] = total

        @pl.loop(0, BLOCK, unroll=2)
        def _(e):
            slot = first + e
            added = [terms[t, pl.ds(e, 1), :] for t in range(TILES)]
            places = [[idx_s[LANE_SETS * t + g, slot] for t in range(TILES)] for g in range(LANE_SETS)]
            held = [[accs[g][pl.ds(places[g][t], 1), :] for t in range(TILES)] for g in range(LANE_SETS)]
            for t in range(TILES):
                for g in range(LANE_SETS):
                    accs[g][pl.ds(places[g][t], 1), :] = held[g][t] + added[t]

    quarter = lax.broadcasted_iota(jnp.int32, (LANES, LANES), 1) >> 5

    def summed(at):
        rows = accs[0][pl.ds(at, LANES), :]
        for g in range(1, LANE_SETS):
            rows = jnp.where(quarter == g, accs[g][pl.ds(at, LANES), :], rows)
        rows = rows.T
        return (rows[:32] + rows[32:64]) + (rows[64:96] + rows[96:])

    @pl.loop(0, owned // LANES)
    def _(b):
        at = pl.multiple_of(b * LANES, LANES)
        both = summed(at)
        curl_out[:, pl.ds(at, LANES)] = both[:ROWS]
        mass_out[:, pl.ds(at, LANES)] = both[ROWS:]

    @pl.loop(0, face // LANES)
    def _(b):
        at = pl.multiple_of(b * LANES, LANES)
        both = summed(owned + at)
        for op in range(2):
            real, imag = both[ROWS * op : ROWS * op + 8], both[ROWS * op + 8 : ROWS * op + ROWS]
            side_x_out[ROWS * op : ROWS * op + 8, pl.ds(at, LANES)] = cosine * real + sine * imag
            side_x_out[ROWS * op + 8 : ROWS * op + ROWS, pl.ds(at, LANES)] = cosine * imag - sine * real
        side_y_out[:, pl.ds(at, LANES)] = summed(owned + face + at)

    total = jnp.zeros((ROWS, LANES), jnp.float32)
    for j in range(NLOC):
        t = j // LANE_SETS
        piece = gram[j * ROWS : (j + 1) * ROWS, t * LANES : (t + 1) * LANES]
        lanes = lax.broadcasted_iota(jnp.int32, (ROWS, LANES), 1) >> 5
        total = total + jnp.where(lanes == j % LANE_SETS, piece, 0.0)
    gram_out[...] = total


def prepare(wraps, dofs, pairing, stiff_mat, mass_mat):
    shape = jax.ShapeDtypeStruct
    wide = (GTILES * LANES, TILES * LANES)
    return pl.pallas_call(
        prepare_kernel,
        out_shape=(
            shape(dofs.shape, jnp.int32),
            shape(wide, jnp.bfloat16),
            shape(wide, jnp.bfloat16),
        ),
        in_specs=[SMEM, VMEM, VMEM, VMEM, VMEM],
        out_specs=(VMEM, VMEM, VMEM),
        compiler_params=pltpu.CompilerParams(vmem_limit_bytes=16 * 2**20),
        name="prepare",
    )(wraps, dofs, pairing, stiff_mat, mass_mat)


def part_images(count, phase, idx, own, high_x, high_y, stiff, mass, kh, kl):
    shape = jax.ShapeDtypeStruct
    owned, face = own.shape[1], high_x.shape[1]
    extent = owned + 2 * face
    f32 = jnp.float32
    return pl.pallas_call(
        part_kernel,
        out_shape=(
            shape((ROWS, owned), f32),
            shape((ROWS, owned), f32),
            shape((2 * ROWS, face), f32),
            shape((2 * ROWS, face), f32),
            shape((ROWS, LANES), f32),
        ),
        in_specs=[SMEM, SMEM, SMEM] + [VMEM] * 8,
        out_specs=(VMEM,) * 5,
        scratch_shapes=[pltpu.VMEM((extent, LANES), f32)] * 5
        + [
            pltpu.VMEM((GTILES, BLOCK, LANES), f32),
            pltpu.VMEM((TILES, BLOCK, LANES), f32),
            pltpu.VMEM((GTILES * LANES, TILES * LANES), f32),
        ],
        compiler_params=pltpu.CompilerParams(vmem_limit_bytes=56 * 2**20),
        name="part_images",
    )(count, phase, idx, idx, own, high_x, high_y, stiff, mass, kh, kl)


def on_device(
    trial_block,
    stiff_coef,
    mass_coef,
    elem_count,
    elem_dofs,
    pairing,
    bloch_fraction,
    stiff_mat,
    mass_mat,
):
    owned = trial_block.shape[-1]
    face = pairing.shape[0]
    interior = owned - 2 * face
    own = trial_block.reshape(ROWS, owned)
    n_px, n_py = lax.axis_size("px"), lax.axis_size("py")
    down_x = [((a + 1) % n_px, a) for a in range(n_px)]
    down_y = [(b + 1, b) for b in range(n_py - 1)]
    high_x = lax.ppermute(own[:, interior : interior + face], "px", down_x)
    high_y = lax.ppermute(own[:, interior + face :], "py", down_y)

    angle = 2.0 * math.pi * bloch_fraction[0].astype(jnp.float32) / bloch_fraction[1].astype(jnp.float32)
    at_end = lax.axis_index("px") == n_px - 1
    phase = jnp.stack([jnp.where(at_end, jnp.cos(angle), 1.0), jnp.where(at_end, jnp.sin(angle), 0.0)])
    wraps = at_end.astype(jnp.int32).reshape(1)
    idx, kh, kl = prepare(
        wraps, elem_dofs[0, 0].T, pairing.reshape(-1, LANES), stiff_mat, mass_mat
    )
    curl, mass, side_x, side_y, gram = part_images(
        elem_count, phase, idx, own, high_x, high_y, stiff_coef[0], mass_coef[0], kh, kl
    )
    back_x = lax.ppermute(side_x, "px", [(a, (a + 1) % n_px) for a in range(n_px)])
    back_y = lax.ppermute(side_y, "py", [(b, b + 1) for b in range(n_py - 1)])

    def finish(image, add_x, add_y):
        low_x = image[:, interior : interior + face] + add_x
        low_y = image[:, interior + face :] + add_y
        whole = jnp.concatenate([image[:, :interior], low_x, low_y], axis=1)
        return whole.reshape(trial_block.shape)

    curl = finish(curl, back_x[:ROWS], back_y[:ROWS])
    mass = finish(mass, back_x[ROWS:], back_y[ROWS:])

    gram = lax.psum(gram, ("px", "py")) / float(n_px * n_py * owned)
    gram = gram.reshape(2, 8, LANE_SETS, 2, 2, 8).sum(2)
    real = gram[0, :, :, 0] + gram[1, :, :, 1]
    imag = gram[0, :, :, 1] - gram[1, :, :, 0]
    return curl, mass, jnp.stack([real, imag]).transpose(2, 0, 1, 3)


def solution(mesh):
    return jax.shard_map(
        on_device,
        mesh=mesh,
        in_specs=(
            P("px", "py", None, None, None),
            P("px", "py", None),
            P("px", "py", None),
            P("px", "py"),
            P("px", "py", None, None),
            P(),
            P(),
            P(),
            P(),
        ),
        out_specs=(P("px", "py", None, None, None), P("px", "py", None, None, None), P()),
        check_vma=False,
    )
```

profile of v0, /device:TPU:1, one launch (start us, length us, event | category | flops | bytes accessed | tf_op | source)
XLA Modules:
  0.0 207.0 jit_solution(5935504161839077545)
XLA Ops:
  0.6 0.0 copy-start.10
  0.6 1.0 fusion
  1.7 0.0 copy-start.11
  1.7 1.3 collective-permute-start.1
  3.0 8.8 %collective-permute-start = (f32[16,2048]{1,0:T(8,128)S(1)}, f32[16,2048]{1,0:T(8,128)S(1)}, u32[]{:S(2)}, u32[]{:S(2)}) collective-permute-start(f32[16,2048]{1,0:T(8,128)S(1)} %get-tuple-element.32), channel_id=1, source_target_pairs={{16,0},{32,16},{48,32},{64,48},{80,64},{96,80},{112,96},{128,112},... | collective-permute-start | bytes 393224 | tf_op jit(solution)/shard_map/ppermute | solution.py:278
  11.8 0.0 copy-done.11
  11.8 0.6 fusion.1
  14.5 0.0 copy-done.10
  14.5 0.0 copy-start.4
  14.5 0.0 copy-start.5
  14.6 0.0 copy-start.3
  14.6 0.6 copy-done.4
  15.2 0.0 copy-done.5
  15.2 0.0 copy-done.3
  15.3 2.8 %prepare.1 = (s32[20,1024]{1,0:T(8,128)S(1)}, bf16[384,640]{1,0:T(8,128)(2,1)S(1)}, bf16[384,640]{1,0:T(8,128)(2,1)S(1)}) custom-call(s32[1]{0:T(128)} %bitcast.4.wrap_ref, s32[20,1024]{1,0:T(8,128)S(1)} %bitcast.24, s32[16,128]{1,0:T(8,128)S(1)} %bitcast.25, f32[20,20]{1,0:T(8,128)S(1)} %copy-done.3, f32[20,20]{1,0:T(8,128)S(1)} %copy-done.4), custom_call_target="tpu_custom_call" | custom-call | tf_op jit(solution)/shard_map/prepare/pallas_call | solution.py:219
  18.1 0.0 copy-start
  18.1 0.8 copy-done
  18.9 0.0 copy-start.1
  18.9 0.8 copy-done.1
  19.7 0.0 copy-start.2
  19.7 0.6 copy-done.2
  20.3 0.6 pad_maximum_fusion.phase_ref
  20.9 0.0 collective-permute-done.1.high_y_ref
  20.9 0.0 copy-start.8
  20.9 0.0 collective-permute-done.high_x_ref
  20.9 0.0 copy-start.9
  20.9 0.7 copy-done.8
  21.6 0.1 copy-done.9
  21.6 43.2 %part_images.1 = (f32[16,8192]{1,0:T(8,128)}, f32[16,8192]{1,0:T(8,128)}, f32[32,2048]{1,0:T(8,128)}, f32[32,2048]{1,0:T(8,128)}, f32[16,128]{1,0:T(8,128)}) custom-call(s32[1,1]{1,0:T(1,128)S(6)} %copy.21.count_ref, f32[2]{0:T(128)} %pad_maximum_fusion.phase_ref, s32[20,1024]{1,0:T(8,128)} %copy-done.2, s32[20,1024]{1,0:T(8,128)} %copy-done.2, ...), custom_call_target="tpu_custom_call" | custom-call | tf_op jit(solution)/shard_map/part_images/pallas_call | solution.py:238
  64.8 0.0 copy-start.7
  64.8 129.0 %psum.7 = f32[16,128]{1,0:T(8,128)S(1)} all-reduce(f32[16,128]{1,0:T(8,128)} %get-tuple-element.18), channel_id=1, replica_groups=mesh['px'=32,'py'=16] {'px','py'}, use_global_device_ids=true, to_apply=%region_0.1 | all-reduce | flops 2048 | bytes 16384 | tf_op jit(solution)/shard_map/psum | solution.py:303
  193.8 0.2 reshape.75
  194.0 0.1 reduce_sum.9
  194.1 2.3 %collective-permute-start.2 = (f32[32,2048]{1,0:T(8,128)}, f32[32,2048]{1,0:T(8,128)S(1)}, u32[]{:S(2)}, u32[]{:S(2)}) collective-permute-start(f32[32,2048]{1,0:T(8,128)} %get-tuple-element.15), channel_id=1, source_target_pairs={{0,16},{16,32},{32,48},{48,64},{64,80},{80,96},{96,112},{112,128},... | collective-permute-start | bytes 786440 | tf_op jit(solution)/shard_map/ppermute | solution.py:291
  196.4 3.8 %collective-permute-start.3 = (f32[32,2048]{1,0:T(8,128)}, f32[32,2048]{1,0:T(8,128)S(1)}, u32[]{:S(2)}, u32[]{:S(2)}) collective-permute-start(f32[32,2048]{1,0:T(8,128)} %get-tuple-element.16), channel_id=1, source_target_pairs={{0,1},{1,2},{2,3},{3,4},{4,5},{5,6},{6,7},{7,8},{8,9},{9,10},{10,1... | collective-permute-start | bytes 786440 | tf_op jit(solution)/shard_map/ppermute | solution.py:292
  200.3 0.6 copy.15
  200.9 0.0 copy-start.6
  200.9 1.0 slice.58
  201.9 0.0 copy-done.7
  202.0 0.0 collective-permute-done.2
  202.0 3.9 %collective-permute-done.3 = f32[32,2048]{1,0:T(8,128)S(1)} collective-permute-done((f32[32,2048]{1,0:T(8,128)}, f32[32,2048]{1,0:T(8,128)S(1)}, u32[]{:S(2)}, u32[]{:S(2)}) %collective-permute-start.3) | collective-permute-done | bytes 262176 | tf_op jit(solution)/shard_map/ppermute | solution.py:292
  205.9 0.0 copy-done.6
  205.9 0.1 slice_add_fusion.3
  206.0 1.0 maximum_bitcast_fusion
  (6 shorter events, 0.1 us)
Async XLA Ops:
  0.6 13.9 %copy-start.10 = (s32[1,1,1024,20]{2,1,3,0:T(1,128)S(1)}, s32[1,1,1024,20]{2,1,3,0:T(1,128)}, u32[]{:S(2)}) copy-start(s32[1,1,1024,20]{2,1,3,0:T(1,128)} %param.13) | copy-start | bytes 245764
  1.7 10.1 %copy-start.11 = (s32[2]{0:T(128)S(1)}, s32[2]{0:T(128)}, u32[]{:S(2)}) copy-start(s32[2]{0:T(128)} %param.15) | copy-start | bytes 28
  1.7 19.2 %collective-permute-start.1 = (f32[16,2048]{1,0:T(8,128)S(1)}, f32[16,2048]{1,0:T(8,128)S(1)}, u32[]{:S(2)}, u32[]{:S(2)}) collective-permute-start(f32[16,2048]{1,0:T(8,128)S(1)} %get-tuple-element.31), channel_id=1, source_target_pairs={{1,0},{2,1},{3,2},{4,3},{5,4},{6,5},{7,6},{8,7},{9,8},{10,9},{11,1... | collective-permute-start | bytes 393224 | tf_op jit(solution)/shard_map/ppermute | solution.py:279
  3.0 17.9 %collective-permute-start = (f32[16,2048]{1,0:T(8,128)S(1)}, f32[16,2048]{1,0:T(8,128)S(1)}, u32[]{:S(2)}, u32[]{:S(2)}) collective-permute-start(f32[16,2048]{1,0:T(8,128)S(1)} %get-tuple-element.32), channel_id=1, source_target_pairs={{16,0},{32,16},{48,32},{64,48},{80,64},{96,80},{112,96},{128,112},... | collective-permute-start | bytes 393224 | tf_op jit(solution)/shard_map/ppermute | solution.py:278
  14.5 0.7 copy-start.4
  14.5 0.7 copy-start.5
  14.6 0.7 copy-start.3
  18.1 0.8 copy-start
  18.9 0.8 copy-start.1
  19.7 0.7 copy-start.2
  20.9 0.7 copy-start.8
  20.9 0.7 copy-start.9
  64.8 137.1 %copy-start.7 = (f32[16,8192]{1,0:T(8,128)S(1)}, f32[16,8192]{1,0:T(8,128)}, u32[]{:S(2)}) copy-start(f32[16,8192]{1,0:T(8,128)} %get-tuple-element.17) | copy-start | bytes 1572868
  194.1 7.8 %collective-permute-start.2 = (f32[32,2048]{1,0:T(8,128)}, f32[32,2048]{1,0:T(8,128)S(1)}, u32[]{:S(2)}, u32[]{:S(2)}) collective-permute-start(f32[32,2048]{1,0:T(8,128)} %get-tuple-element.15), channel_id=1, source_target_pairs={{0,16},{16,32},{32,48},{48,64},{64,80},{80,96},{96,112},{112,128},... | collective-permute-start | bytes 786440 | tf_op jit(solution)/shard_map/ppermute | solution.py:291
  196.4 9.5 %collective-permute-start.3 = (f32[32,2048]{1,0:T(8,128)}, f32[32,2048]{1,0:T(8,128)S(1)}, u32[]{:S(2)}, u32[]{:S(2)}) collective-permute-start(f32[32,2048]{1,0:T(8,128)} %get-tuple-element.16), channel_id=1, source_target_pairs={{0,1},{1,2},{2,3},{3,4},{4,5},{5,6},{6,7},{7,8},{8,9},{9,10},{10,1... | collective-permute-start | bytes 786440 | tf_op jit(solution)/shard_map/ppermute | solution.py:292
  200.9 5.0 %copy-start.6 = (f32[16,8192]{1,0:T(8,128)S(1)}, f32[16,8192]{1,0:T(8,128)}, u32[]{:S(2)}) copy-start(f32[16,8192]{1,0:T(8,128)} %get-tuple-element.14) | copy-start | bytes 1572868
where the time goes:
time: 210 us; the launch traced here: 207 us
  blocking collectives  129 us (61%)
  Pallas kernels  46 us (22%)
  starting transfers between devices  16.2 us (8%)
  local copies, waits for them, and re-layouts  7.17 us (3%)
  waiting for transfers between devices  3.93 us (2%)
  between operations  2.99 us (1%)
    psum x1, blocking collectives, on_device(): gram = lax.psum(gram, ('px', 'py')) / float(n_px * n_py * owned)  129 us
    pallas_call x1, Pallas kernels, part_images(): pl.pallas_call(part_kernel, out_shape=(shape((ROWS, owned), f32), shape((...  43.2 us
    ppermute x1, starting transfers between devices, on_device(): high_x = lax.ppermute(own[:, interior:interior + face], 'px', down_x)  8.79 us
    unnamed x26, local copies, waits for them, and re-layouts  4.28 us
  transfers between devices with their start and end apart: 4, of which 1 were waited for; matrix products, arithmetic and copies ran while one was open for 1% of the time, Pallas kernels for 1%

commit v1 on v0

--- a/solution.py
+++ b/solution.py
@@ -37,8 +37,10 @@
 def prepare_kernel(wrap_ref, dofs_ref, pairing_ref, stiff_ref, mass_ref, idx_out, kh_out, kl_out):
     face = pairing_ref.shape[0] * LANES
     owned = 4 * face
+    blocks = dofs_ref.shape[0] // NLOC
     idx_out[...] = dofs_ref[...]
-    head = dofs_ref[:, :HALO_SLOTS]
+    heads = pl.ds(0, NLOC, stride=blocks)
+    head = dofs_ref[heads, :]
     spot = head - owned
     local = spot & (LANES - 1)
     found = jnp.zeros_like(head)
@@ -47,7 +49,7 @@
         here = jnp.take_along_axis(values, local, axis=1)
         found = jnp.where((spot >> 7) == row, here + owned, found)
     wraps = (spot >= 0) & (spot < face) & (wrap_ref[0] == 1)
-    idx_out[:, :HALO_SLOTS] = jnp.where(wraps, found, head)
+    idx_out[heads, :] = jnp.where(wraps, found, head)
 
     grow = lax.broadcasted_iota(jnp.int32, (GTILES * LANES, NLOC), 0)
     gcol = lax.broadcasted_iota(jnp.int32, (GTILES * LANES, NLOC), 1)
@@ -96,16 +98,18 @@
     face = high_x_ref.shape[1]
     cosine, sine = phase_ref[0], phase_ref[1]
     count = count_ref[0, 0]
+    capacity = stiff_ref.shape[1]
+    blocks = capacity // BLOCK
 
     def put_rows(at, block):
         ext[pl.ds(at, LANES), :] = jnp.concatenate([block] * (LANES // ROWS), axis=0).T
 
-    @pl.loop(0, owned // LANES)
+    @pl.loop(0, owned // LANES, unroll=8)
     def _(b):
         at = pl.multiple_of(b * LANES, LANES)
         put_rows(at, own_ref[:, pl.ds(at, LANES)])
 
-    @pl.loop(0, face // LANES)
+    @pl.loop(0, face // LANES, unroll=4)
     def _(b):
         at = pl.multiple_of(b * LANES, LANES)
         got = high_x_ref[:, pl.ds(at, LANES)]
@@ -136,7 +140,7 @@
                 inside = range(8 * tile, min(8 * tile + 8, NLOC))
                 row = None
                 for i in inside:
-                    got = ext[pl.ds(idx_s[i, slot], 1), :]
+                    got = ext[pl.ds(idx_s[slot + i * capacity], 1), :]
                     row = got if row is None else jnp.where(lane_set == i % 8, got, row)
                 gathered[tile, pl.ds(e, 1), :] = row
 
@@ -158,7 +162,7 @@
         names = []
         for t in range(TILES):
             rows = [
-                jnp.broadcast_to(idx_v[j : j + 1, pl.ds(first, BLOCK)], (LANES // LANE_SETS, BLOCK))
+                jnp.broadcast_to(idx_v[pl.ds(j * blocks + block_id, 1), :], (LANES // LANE_SETS, BLOCK))
                 for j in range(LANE_SETS * t, LANE_SETS * t + LANE_SETS)
             ]
             names.append(jnp.concatenate(rows, axis=0).astype(jnp.float32).T)
@@ -172,7 +176,7 @@
         def _(e):
             slot = first + e
             added = [terms[t, pl.ds(e, 1), :] for t in range(TILES)]
-            places = [[idx_s[LANE_SETS * t + g, slot] for t in range(TILES)] for g in range(LANE_SETS)]
+            places = [[idx_s[slot + (LANE_SETS * t + g) * capacity] for t in range(TILES)] for g in range(LANE_SETS)]
             held = [[accs[g][pl.ds(places[g][t], 1), :] for t in range(TILES)] for g in range(LANE_SETS)]
             for t in range(TILES):
                 for g in range(LANE_SETS):
@@ -187,14 +191,14 @@
         rows = rows.T
         return (rows[:32] + rows[32:64]) + (rows[64:96] + rows[96:])
 
-    @pl.loop(0, owned // LANES)
+    @pl.loop(0, owned // LANES, unroll=4)
     def _(b):
         at = pl.multiple_of(b * LANES, LANES)
         both = summed(at)
         curl_out[:, pl.ds(at, LANES)] = both[:ROWS]
         mass_out[:, pl.ds(at, LANES)] = both[ROWS:]
 
-    @pl.loop(0, face // LANES)
+    @pl.loop(0, face // LANES, unroll=2)
     def _(b):
         at = pl.multiple_of(b * LANES, LANES)
         both = summed(owned + at)
@@ -210,7 +214,157 @@
         piece = gram[j * ROWS : (j + 1) * ROWS, t * LANES : (t + 1) * LANES]
         lanes = lax.broadcasted_iota(jnp.int32, (ROWS, LANES), 1) >> 5
         total = total + jnp.where(lanes == j % LANE_SETS, piece, 0.0)
-    gram_out[...] = total
+    for shift in (LANES // 2, LANES // 4):
+        total = total + pltpu.roll(total, shift, 1)
+    of_real, of_imag = total[:8], total[8:]
+    odd = ((lax.broadcasted_iota(jnp.int32, (8, LANES), 1) >> 3) & 1) == 1
+    gram_out[...] = jnp.where(
+        odd, of_real - pltpu.roll(of_imag, 8, 1), of_real + pltpu.roll(of_imag, LANES - 8, 1)
+    )
+
+
+def exchange_kernel(
+    side_x_ref,
+    side_y_ref,
+    gram_ref,
+    back_x,
+    back_y,
+    gram_out,
+    along_x,
+    row_sum,
+    along_y,
+    side_send,
+    side_recv,
+    send_x,
+    recv_x,
+    send_y,
+    recv_y,
+):
+    n_px, n_py = along_x.shape[0], along_y.shape[0]
+    a, b = lax.axis_index("px"), lax.axis_index("py")
+
+    barrier = pltpu.get_barrier_semaphore()
+
+    def greet(axis, me, n):
+        @pl.loop(1, n)
+        def _(k):
+            other = lax.rem(me + k, n)
+            pl.semaphore_signal(barrier, 1, device_id={axis: other}, device_id_type=pl.DeviceIdType.MESH)
+
+    greet("px", a, n_px)
+    greet("py", b, n_py)
+    pl.semaphore_wait(barrier, n_px + n_py - 2)
+
+    def tile_copy(axis, to, source, held, at, send, recv):
+        return pltpu.make_async_remote_copy(
+            src_ref=source,
+            dst_ref=held.at[at],
+            send_sem=send.at[to],
+            recv_sem=recv.at[at],
+            device_id={axis: to},
+            device_id_type=pl.DeviceIdType.MESH,
+        )
+
+    def send_all(axis, me, n, source, held, send, recv):
+        @pl.loop(1, n)
+        def _(k):
+            tile_copy(axis, lax.rem(me + k, n), source, held, me, send, recv).start()
+
+    def sum_all(axis, me, n, source, held, send, recv):
+        held[pl.ds(me, 1)] = source[...][None]
+
+        @pl.loop(1, n)
+        def _(k):
+            other = lax.rem(me + k, n)
+            tile_copy(axis, other, source, held, other, send, recv).wait_recv()
+
+        total = held[0]
+        for at in range(1, n):
+            total = total + held[at]
+        return total
+
+    def sent_all(axis, me, n, source, held, send, recv):
+        @pl.loop(1, n)
+        def _(k):
+            tile_copy(axis, lax.rem(me + k, n), source, held, me, send, recv).wait_send()
+
+    def side_copy(source, held, at, axis, to):
+        return pltpu.make_async_remote_copy(
+            src_ref=source,
+            dst_ref=held,
+            send_sem=side_send.at[at],
+            recv_sem=side_recv.at[at],
+            device_id={axis: to},
+            device_id_type=pl.DeviceIdType.MESH,
+        )
+
+    over_x = ("px", a, n_px, gram_ref, along_x, send_x, recv_x)
+    over_y = ("py", b, n_py, row_sum, along_y, send_y, recv_y)
+    to_x = side_copy(side_x_ref, back_x, 0, "px", lax.rem(a + 1, n_px))
+    to_y = side_copy(side_y_ref, back_y, 1, "py", lax.rem(b + 1, n_py))
+    send_all(*over_x)
+    to_x.start()
+
+    @pl.when(b < n_py - 1)
+    def _():
+        to_y.start()
+
+    row_sum[...] = sum_all(*over_x)
+    send_all(*over_y)
+    whole = sum_all(*over_y)
+    for op in range(2):
+        for part in range(2):
+            at = 16 * op + 8 * part
+            gram_out[op, part] = whole[:, at : at + 8] / gram_scale(n_px, n_py, side_x_ref)
+    to_x.wait_recv()
+
+    @pl.when(b > 0)
+    def _():
+        to_y.wait_recv()
+
+    @pl.when(b == 0)
+    def _():
+        back_y[...] = jnp.zeros_like(back_y)
+
+    to_x.wait_send()
+
+    @pl.when(b < n_py - 1)
+    def _():
+        to_y.wait_send()
+
+    sent_all(*over_x)
+    sent_all(*over_y)
+
+
+def gram_scale(n_px, n_py, side_ref):
+    return float(n_px * n_py * 4 * side_ref.shape[1])
+
+
+def exchange(side_x, side_y, gram, n_px, n_py):
+    shape = jax.ShapeDtypeStruct
+    f32 = jnp.float32
+    dma = pltpu.SemaphoreType.DMA
+    return pl.pallas_call(
+        exchange_kernel,
+        out_shape=(shape(side_x.shape, f32), shape(side_y.shape, f32), shape((2, 2, 8, 8), f32)),
+        in_specs=[VMEM] * 3,
+        out_specs=(VMEM,) * 3,
+        scratch_shapes=[
+            pltpu.VMEM((n_px, 8, LANES), f32),
+            pltpu.VMEM((8, LANES), f32),
+            pltpu.VMEM((n_py, 8, LANES), f32),
+            dma((2,)),
+            dma((2,)),
+            dma((n_px,)),
+            dma((n_px,)),
+            dma((n_py,)),
+            dma((n_py,)),
+        ],
+        compiler_params=pltpu.CompilerParams(
+            collective_id=0, has_side_effects=True, vmem_limit_bytes=16 * 2**20
+        ),
+        name="exchange",
+    )(side_x, side_y, gram)
 
 
 def prepare(wraps, dofs, pairing, stiff_mat, mass_mat):
@@ -242,7 +396,7 @@
             shape((ROWS, owned), f32),
             shape((2 * ROWS, face), f32),
             shape((2 * ROWS, face), f32),
-            shape((ROWS, LANES), f32),
+            shape((8, LANES), f32),
         ),
         in_specs=[SMEM, SMEM, SMEM] + [VMEM] * 8,
         out_specs=(VMEM,) * 5,
@@ -254,7 +408,7 @@
         ],
         compiler_params=pltpu.CompilerParams(vmem_limit_bytes=56 * 2**20),
         name="part_images",
-    )(count, phase, idx, idx, own, high_x, high_y, stiff, mass, kh, kl)
+    )(count, phase, idx.reshape(-1), idx, own, high_x, high_y, stiff, mass, kh, kl)
 
 
 def on_device(
@@ -283,13 +437,12 @@
     phase = jnp.stack([jnp.where(at_end, jnp.cos(angle), 1.0), jnp.where(at_end, jnp.sin(angle), 0.0)])
     wraps = at_end.astype(jnp.int32).reshape(1)
     idx, kh, kl = prepare(
-        wraps, elem_dofs[0, 0].T, pairing.reshape(-1, LANES), stiff_mat, mass_mat
+        wraps, elem_dofs[0, 0].T.reshape(-1, LANES), pairing.reshape(-1, LANES), stiff_mat, mass_mat
     )
     curl, mass, side_x, side_y, gram = part_images(
         elem_count, phase, idx, own, high_x, high_y, stiff_coef[0], mass_coef[0], kh, kl
     )
-    back_x = lax.ppermute(side_x, "px", [(a, (a + 1) % n_px) for a in range(n_px)])
-    back_y = lax.ppermute(side_y, "py", [(b, b + 1) for b in range(n_py - 1)])
+    back_x, back_y, gram = exchange(side_x, side_y, gram, n_px, n_py)
 
     def finish(image, add_x, add_y):
         low_x = image[:, interior : interior + face] + add_x
@@ -299,12 +452,7 @@
 
     curl = finish(curl, back_x[:ROWS], back_y[:ROWS])
     mass = finish(mass, back_x[ROWS:], back_y[ROWS:])
-
-    gram = lax.psum(gram, ("px", "py")) / float(n_px * n_py * owned)
-    gram = gram.reshape(2, 8, LANE_SETS, 2, 2, 8).sum(2)
-    real = gram[0, :, :, 0] + gram[1, :, :, 1]
-    imag = gram[0, :, :, 1] - gram[1, :, :, 0]
-    return curl, mass, jnp.stack([real, imag]).transpose(2, 0, 1, 3)
+    return curl, mass, gram
 
 
 def solution(mesh):

time: 210 us -> 100 us (0.48); the launches traced: 207 us -> 99.9 us
  blocking collectives: 129 us -> 0 us
  Pallas kernels: 46 us -> 77.2 us
  starting transfers between devices: 16.2 us -> 10.1 us
  waiting for transfers between devices: 3.93 us -> 0.01 us
    psum x1 -> x0, blocking collectives: 129 us -> none  [on_device(): gram = lax.psum(gram, ('px', 'py')) / float(n_px * n_py * owned)]
    pallas_call x0 -> x1, Pallas kernels: none -> 46 us  [exchange(): pl.pallas_call(exchange_kernel, out_shape=(shape(side_x.shape, f32), shap...]
    pallas_call x1, Pallas kernels: 43.2 us -> 28.4 us  [part_images(): pl.pallas_call(part_kernel, out_shape=(shape((ROWS, owned), f32), shape((...]
    ppermute x2 -> x0, starting transfers between devices: 6.1 us -> none  [the longest x1 3.81 us: on_device(): back_y = lax.ppermute(side_y, 'py', [(b, b + 1) for b in range(n_py - 1)])]
    ppermute x2 -> x0, waiting for transfers between devices: 3.93 us -> none  [the longest x1 3.92 us: on_device(): back_y = lax.ppermute(side_y, 'py', [(b, b + 1) for b in range(n_py - 1)])]
    unnamed x26 -> x32, local copies, waits for them, and re-layouts: 4.28 us -> 5.3 us
  transfers between devices with their start and end apart: 4 -> 2, of which waited for: 1 -> 0; matrix products, arithmetic and copies ran while one was open for 1% -> 1% of each run, Pallas kernels for 1% -> 3%
where the time goes in v1:
time: 100 us; the launch traced here: 99.9 us
  Pallas kernels  77.2 us (77%)
  starting transfers between devices  10.1 us (10%)
  local copies, waits for them, and re-layouts  7.97 us (8%)
  between operations  2.95 us (3%)
  other arithmetic  1.75 us (2%)
    pallas_call x1, Pallas kernels, exchange(): pl.pallas_call(exchange_kernel, out_shape=(shape(side_x.shape, f32), shap...  46 us
    pallas_call x1, Pallas kernels, part_images(): pl.pallas_call(part_kernel, out_shape=(shape((ROWS, owned), f32), shape((...  28.4 us
    ppermute x1, starting transfers between devices, on_device(): high_x = lax.ppermute(own[:, interior:interior + face], 'px', down_x)  8.79 us
    unnamed x32, local copies, waits for them, and re-layouts  5.3 us
    pallas_call x1, Pallas kernels, prepare(): pl.pallas_call(prepare_kernel, out_shape=(shape(dofs.shape, jnp.int32), s...  2.79 us
  transfers between devices with their start and end apart: 2, of which 0 were waited for; matrix products, arithmetic and copies ran while one was open for 1% of the time, Pallas kernels for 3%

profile of v1, /device:TPU:1, one launch (start us, length us, event | category | flops | bytes accessed | tf_op | source)
XLA Modules:
  0.0 99.9 jit_solution(821863327355275467)
XLA Ops:
  0.6 0.0 copy-start.13
  0.6 1.0 %fusion = (f32[16,2048]{1,0:T(8,128)S(1)}, f32[16,2048]{1,0:T(8,128)S(1)}) fusion(f32[16,8192]{1,0:T(8,128)} %bitcast.21), kind=kLoop, calls=%fused_computation.8 | loop fusion | bytes 524288 | tf_op jit(solution)/shard_map/slice | solution.py:433
  1.7 0.0 copy-start.14
  1.7 1.3 %collective-permute-start.1 = (f32[16,2048]{1,0:T(8,128)S(1)}, f32[16,2048]{1,0:T(8,128)S(1)}, u32[]{:S(2)}, u32[]{:S(2)}) collective-permute-start(f32[16,2048]{1,0:T(8,128)S(1)} %get-tuple-element.31), channel_id=1, source_target_pairs={{1,0},{2,1},{3,2},{4,3},{5,4},{6,5},{7,6},{8,7},{9,8},{10,9},{11,1... | collective-permute-start | bytes 393224 | tf_op jit(solution)/shard_map/ppermute | solution.py:433
  3.0 8.8 %collective-permute-start = (f32[16,2048]{1,0:T(8,128)S(1)}, f32[16,2048]{1,0:T(8,128)S(1)}, u32[]{:S(2)}, u32[]{:S(2)}) collective-permute-start(f32[16,2048]{1,0:T(8,128)S(1)} %get-tuple-element.32), channel_id=1, source_target_pairs={{16,0},{32,16},{48,32},{64,48},{80,64},{96,80},{112,96},{128,112},... | collective-permute-start | bytes 393224 | tf_op jit(solution)/shard_map/ppermute | solution.py:432
  11.8 0.0 copy-done.14
  11.8 0.6 fusion.1
  14.5 0.0 copy-done.13
  14.5 0.0 copy-start.5
  14.6 0.0 copy-start.6
  14.6 0.0 copy-start.7
  14.6 0.6 copy-done.5
  15.3 0.0 copy-done.6
  15.3 0.0 copy-done.7
  15.3 2.8 %prepare.1 = (s32[160,128]{1,0:T(8,128)S(1)}, bf16[384,640]{1,0:T(8,128)(2,1)S(1)}, bf16[384,640]{1,0:T(8,128)(2,1)S(1)}) custom-call(s32[1]{0:T(128)} %bitcast.4.wrap_ref, s32[160,128]{1,0:T(8,128)S(1)} %reshape.38.dofs_ref, s32[16,128]{1,0:T(8,128)S(1)} %bitcast.20, f32[20,20]{1,0:T(8,128)S(1)} %copy-done.5, f32[20,20]{1,0:T(8,128)S(1)} %copy-done.6), custom_call_target="tpu_custom_call" | custom-call | tf_op jit(solution)/shard_map/prepare/pallas_call | solution.py:373
  18.1 0.0 copy-start
  18.1 0.8 copy-done
  18.9 0.0 copy-start.1
  18.9 0.8 copy-done.1
  19.7 0.0 copy-start.2
  19.7 0.6 copy-done.2
  20.3 0.7 pad_maximum_fusion.phase_ref
  21.0 0.0 collective-permute-done.1.high_y_ref
  21.0 0.0 copy-start.11
  21.0 0.0 collective-permute-done.high_x_ref
  21.0 0.0 copy-start.12
  21.0 0.6 copy-done.11
  21.6 0.1 copy-done.12
  21.7 28.4 %part_images.1 = (f32[16,8192]{1,0:T(8,128)}, f32[16,8192]{1,0:T(8,128)}, f32[32,2048]{1,0:T(8,128)}, f32[32,2048]{1,0:T(8,128)}, f32[8,128]{1,0:T(8,128)}) custom-call(s32[1,1]{1,0:T(1,128)S(6)} %copy.16.count_ref, f32[2]{0:T(128)} %pad_maximum_fusion.phase_ref, s32[20480]{0:T(1024)} %bitcast.19, s32[160,128]{1,0:T(8,128)} %copy-done.2, ...), custom_call_target="tpu_custom_call" | custom-call | tf_op jit(solution)/shard_map/part_images/pallas_call | solution.py:392
  50.1 0.0 copy-start.9
  50.1 1.0 %slice.51 = f32[16,4096]{1,0:T(8,128)S(1)} slice(f32[16,8192]{1,0:T(8,128)} %get-tuple-element.23), slice={[0:16], [0:4096]} | slice | bytes 524288 | tf_op jit(solution)/shard_map/slice | solution.py:450
  51.1 0.1 copy-done.9
  51.2 0.0 copy-start.3
  51.2 0.0 copy-start.4
  51.2 0.0 copy-start.8
  51.2 0.0 copy-start.10
  51.2 0.9 copy-done.3
  52.1 0.1 copy-done.4
  52.2 0.0 copy-done.8
  52.2 46.0 %exchange.1 = (f32[32,2048]{1,0:T(8,128)S(1)}, f32[32,2048]{1,0:T(8,128)S(1)}, f32[2,2,8,8]{3,2,1,0:T(8,128)S(1)}) custom-call(f32[32,2048]{1,0:T(8,128)S(1)} %copy-done.3, f32[32,2048]{1,0:T(8,128)S(1)} %copy-done.4, f32[8,128]{1,0:T(8,128)S(1)} %copy-done.8), custom_call_target="tpu_custom_call" | custom-call | tf_op jit(solution)/shard_map/exchange/pallas_call | solution.py:347
  98.2 0.0 copy-done.10
  98.2 0.1 slice_add_fusion.3
  98.3 1.0 %maximum_bitcast_fusion = (f32[1,1,2,8,8192]{4,3,2,1,0:T(8,128)}, f32[1,1,2,8,8192]{4,3,2,1,0:T(8,128)}) fusion(f32[16,2048]{1,0:T(8,128)S(1)} %get-tuple-element.28, f32[16,2048]{1,0:T(8,128)S(1)} %get-tuple-element.27, f32[16,4096]{1,0:T(8,128)S(1)} %slice.46, f32[16,2048]{1,0:T(8,128)S(1)} %get-tuple-element.29, f32[16,2048]{1,0:T(8,128)S(1)} %get-tuple-element.30, ...), kind=kLoop, calls=%fused_computation | loop fusion | flops 524288 | bytes 2097152 | tf_op jit(solution)/shard_map/reshape | solution.py:451
  99.3 0.6 copy.17
  (3 shorter events, 0.1 us)
Async XLA Ops:
  0.6 13.9 %copy-start.13 = (s32[1,1,1024,20]{2,1,3,0:T(1,128)S(1)}, s32[1,1,1024,20]{2,1,3,0:T(1,128)}, u32[]{:S(2)}) copy-start(s32[1,1,1024,20]{2,1,3,0:T(1,128)} %param.13) | copy-start | bytes 245764
  1.7 10.1 %copy-start.14 = (s32[2]{0:T(128)S(1)}, s32[2]{0:T(128)}, u32[]{:S(2)}) copy-start(s32[2]{0:T(128)} %param.15) | copy-start | bytes 28
  1.7 19.3 %collective-permute-start.1 = (f32[16,2048]{1,0:T(8,128)S(1)}, f32[16,2048]{1,0:T(8,128)S(1)}, u32[]{:S(2)}, u32[]{:S(2)}) collective-permute-start(f32[16,2048]{1,0:T(8,128)S(1)} %get-tuple-element.31), channel_id=1, source_target_pairs={{1,0},{2,1},{3,2},{4,3},{5,4},{6,5},{7,6},{8,7},{9,8},{10,9},{11,1... | collective-permute-start | bytes 393224 | tf_op jit(solution)/shard_map/ppermute | solution.py:433
  3.0 18.0 %collective-permute-start = (f32[16,2048]{1,0:T(8,128)S(1)}, f32[16,2048]{1,0:T(8,128)S(1)}, u32[]{:S(2)}, u32[]{:S(2)}) collective-permute-start(f32[16,2048]{1,0:T(8,128)S(1)} %get-tuple-element.32), channel_id=1, source_target_pairs={{16,0},{32,16},{48,32},{64,48},{80,64},{96,80},{112,96},{128,112},... | collective-permute-start | bytes 393224 | tf_op jit(solution)/shard_map/ppermute | solution.py:432
  14.5 0.7 copy-start.5
  14.6 0.7 copy-start.6
  14.6 0.7 copy-start.7
  18.1 0.8 copy-start
  18.9 0.8 copy-start.1
  19.7 0.6 copy-start.2
  21.0 0.7 copy-start.11
  21.0 0.7 copy-start.12
  50.1 1.1 %copy-start.9 = (f32[16,8192]{1,0:T(8,128)S(1)}, f32[16,8192]{1,0:T(8,128)}, u32[]{:S(2)}) copy-start(f32[16,8192]{1,0:T(8,128)} %get-tuple-element.17) | copy-start | bytes 1572868
  51.2 0.9 copy-start.3
  51.2 1.0 %copy-start.4 = (f32[32,2048]{1,0:T(8,128)S(1)}, f32[32,2048]{1,0:T(8,128)}, u32[]{:S(2)}) copy-start(f32[32,2048]{1,0:T(8,128)} %get-tuple-element.19.side_y_ref) | copy-start | bytes 786436
  51.2 1.0 %copy-start.8 = (f32[8,128]{1,0:T(8,128)S(1)}, f32[8,128]{1,0:T(8,128)}, u32[]{:S(2)}) copy-start(f32[8,128]{1,0:T(8,128)} %get-tuple-element.20.gram_ref) | copy-start | bytes 12292
  51.2 47.0 %copy-start.10 = (f32[16,8192]{1,0:T(8,128)S(1)}, f32[16,8192]{1,0:T(8,128)}, u32[]{:S(2)}) copy-start(f32[16,8192]{1,0:T(8,128)} %get-tuple-element.23) | copy-start | bytes 1572868

commit v2 on v1

--- a/solution.py
+++ b/solution.py
@@ -13,13 +13,16 @@
 ROWS = 16
 NLOC = 20
 HALO_SLOTS = 128
-BLOCK = 128
+BLOCK = 256
 TILES = 5
 GTILES = 3
 LANE_SETS = 4
 
 VMEM = pl.BlockSpec(memory_space=pltpu.VMEM)
 SMEM = pl.BlockSpec(memory_space=pltpu.SMEM)
+ANY = pl.BlockSpec(memory_space=pl.ANY)
+VMEM_BYTES = 56 * 2**20
+OUT_CHUNKS = 2
 
 
 def split_bf16(value):
@@ -31,12 +34,83 @@
 def dot_split(a, b):
     (ah, al), (bh, bl) = a, b
     dot = functools.partial(jnp.dot, preferred_element_type=jnp.float32)
-    return dot(ah, bh) + (dot(al, bh) + dot(ah, bl))
-
-
-def prepare_kernel(wrap_ref, dofs_ref, pairing_ref, stiff_ref, mass_ref, idx_out, kh_out, kl_out):
+    both = dot(jnp.concatenate([ah, al], axis=0), bh)
+    rows = ah.shape[0]
+    return both[:rows] + (both[rows:] + dot(ah, bl))
+
+
+def begin_kernel(
+    fraction_ref,
+    own_hbm,
+    dofs_ref,
+    pairing_ref,
+    stiff_ref,
+    mass_ref,
+    high_x,
+    high_y,
+    phase_out,
+    idx_out,
+    kh_out,
+    kl_out,
+    zeros,
+    sems,
+):
     face = pairing_ref.shape[0] * LANES
-    owned = 4 * face
+    owned = own_hbm.shape[1]
+    n_px, n_py = lax.axis_size("px"), lax.axis_size("py")
+    a, b = lax.axis_index("px"), lax.axis_index("py")
+    below_x, above_x = lax.rem(a + n_px - 1, n_px), lax.rem(a + 1, n_px)
+    below_y, above_y = lax.rem(b + n_py - 1, n_py), lax.rem(b + 1, n_py)
+
+    barrier = pltpu.get_barrier_semaphore()
+
+    def greet(axis, to):
+        pl.semaphore_signal(barrier, 1, device_id={axis: to}, device_id_type=pl.DeviceIdType.MESH)
+
+    greet("px", below_x)
+    greet("px", above_x)
+
+    @pl.when(b > 0)
+    def _():
+        greet("py", below_y)
+
+    @pl.when(b < n_py - 1)
+    def _():
+        greet("py", above_y)
+
+    pl.semaphore_wait(barrier, 2 + jnp.minimum(b, 1) + jnp.minimum(n_py - 1 - b, 1))
+
+    def face_copy(first, target, at, axis, to):
+        return pltpu.make_async_remote_copy(
+            src_ref=own_hbm.at[:, pl.ds(first, face)],
+            dst_ref=target,
+            send_sem=sems.at[2 * at],
+            recv_sem=sems.at[2 * at + 1],
+            device_id={axis: to},
+            device_id_type=pl.DeviceIdType.MESH,
+        )
+
+    to_x = face_copy(owned - 2 * face, high_x, 0, "px", below_x)
+    to_y = face_copy(owned - face, high_y, 1, "py", below_y)
+    no_y = pltpu.make_async_copy(zeros, high_y, sems.at[4])
+    to_x.start()
+
+    @pl.when(b > 0)
+    def _():
+        to_y.start()
+
+    @pl.when(b == n_py - 1)
+    def _():
+        zeros[...] = jnp.zeros_like(zeros)
+        no_y.start()
+
+    at_end = jnp.broadcast_to(a, (1, LANES)) == n_px - 1
+    above = jnp.broadcast_to(fraction_ref[0], (1, LANES)).astype(jnp.float32)
+    below = jnp.broadcast_to(fraction_ref[1], (1, LANES)).astype(jnp.float32)
+    angle = 2.0 * math.pi * above / below
+    phase_out[0:1, :] = jnp.where(at_end, jnp.cos(angle), 1.0)
+    phase_out[1:2, :] = jnp.where(at_end, jnp.sin(angle), 0.0)
+
     blocks = dofs_ref.shape[0] // NLOC
     idx_out[...] = dofs_ref[...]
     heads = pl.ds(0, NLOC, stride=blocks)
@@ -48,7 +122,7 @@
         values = jnp.broadcast_to(pairing_ref[row : row + 1, :], head.shape)
         here = jnp.take_along_axis(values, local, axis=1)
         found = jnp.where((spot >> 7) == row, here + owned, found)
-    wraps = (spot >= 0) & (spot < face) & (wrap_ref[0] == 1)
+    wraps = (spot >= 0) & (spot < face) & (jnp.broadcast_to(a, head.shape) == n_px - 1)
     idx_out[heads, :] = jnp.where(wraps, found, head)
 
     grow = lax.broadcasted_iota(jnp.int32, (GTILES * LANES, NLOC), 0)
@@ -66,15 +140,49 @@
     both = jnp.where((krow & 15) == (kcol & 15), both, 0.0)
     kh_out[...], kl_out[...] = split_bf16(both)
 
+    to_x.wait()
+
+    @pl.when(b > 0)
+    def _():
+        to_y.wait_send()
+
+    @pl.when(b < n_py - 1)
+    def _():
+        to_y.wait_recv()
+
+    @pl.when(b == n_py - 1)
+    def _():
+        no_y.wait()
+
+
+def begin(fraction, own, dofs, pairing, stiff_mat, mass_mat):
+    shape = jax.ShapeDtypeStruct
+    high = shape((ROWS, pairing.size), jnp.float32)
+    spread = shape((GTILES * LANES, TILES * LANES), jnp.bfloat16)
+    return pl.pallas_call(
+        begin_kernel,
+        out_shape=(high, high, shape((2, LANES), jnp.float32), shape(dofs.shape, jnp.int32), spread, spread),
+        in_specs=[SMEM, ANY, VMEM, VMEM, VMEM, VMEM],
+        out_specs=(ANY, ANY, VMEM, VMEM, VMEM, VMEM),
+        scratch_shapes=[
+            pltpu.VMEM(high.shape, jnp.float32),
+            pltpu.SemaphoreType.DMA((5,)),
+        ],
+        compiler_params=pltpu.CompilerParams(
+            collective_id=1, has_side_effects=True, vmem_limit_bytes=VMEM_BYTES
+        ),
+        name="begin",
+    )(fraction, own, dofs, pairing, stiff_mat, mass_mat)
+
 
 def part_kernel(
     count_ref,
+    idx_hbm,
+    own_hbm,
+    high_x_hbm,
+    high_y_hbm,
     phase_ref,
-    idx_s,
     idx_v,
-    own_ref,
-    high_x_ref,
-    high_y_ref,
     stiff_ref,
     mass_ref,
     kh_ref,
@@ -92,31 +200,29 @@
     gathered,
     terms,
     gram,
+    idx_all,
+    own_v,
+    high_v,
+    images,
+    in_sems,
+    out_sems,
 ):
     accs = (acc0, acc1, acc2, acc3)
-    owned = own_ref.shape[1]
-    face = high_x_ref.shape[1]
-    cosine, sine = phase_ref[0], phase_ref[1]
+    owned = own_v.shape[1]
+    face = high_v.shape[2]
+    cosine, sine = phase_ref[0:1, :], phase_ref[1:2, :]
     count = count_ref[0, 0]
     capacity = stiff_ref.shape[1]
-    blocks = capacity // BLOCK
-
-    def put_rows(at, block):
-        ext[pl.ds(at, LANES), :] = jnp.concatenate([block] * (LANES // ROWS), axis=0).T
-
-    @pl.loop(0, owned // LANES, unroll=8)
-    def _(b):
-        at = pl.multiple_of(b * LANES, LANES)
-        put_rows(at, own_ref[:, pl.ds(at, LANES)])
-
-    @pl.loop(0, face // LANES, unroll=4)
-    def _(b):
-        at = pl.multiple_of(b * LANES, LANES)
-        got = high_x_ref[:, pl.ds(at, LANES)]
-        real, imag = got[: ROWS // 2], got[ROWS // 2 :]
-        turned = jnp.concatenate([cosine * real - sine * imag, sine * real + cosine * imag], axis=0)
-        put_rows(owned + at, turned)
-        put_rows(owned + face + at, high_y_ref[:, pl.ds(at, LANES)])
+    idx_s = [idx_all.at[pl.ds(j * capacity, capacity)] for j in range(NLOC)]
+
+    own_in = pltpu.make_async_copy(own_hbm, own_v, in_sems.at[0])
+    high_x_in = pltpu.make_async_copy(high_x_hbm, high_v.at[0], in_sems.at[1])
+    high_y_in = pltpu.make_async_copy(high_y_hbm, high_v.at[1], in_sems.at[2])
+    idx_in = pltpu.make_async_copy(idx_hbm, idx_all, in_sems.at[3])
+    own_in.start()
+    idx_in.start()
+    high_x_in.start()
+    high_y_in.start()
 
     zero_rows = jnp.zeros((LANES, LANES), jnp.float32)
 
@@ -127,7 +233,36 @@
             acc[pl.ds(at, LANES), :] = zero_rows
 
     gram[...] = jnp.zeros_like(gram)
+
+    def put_rows(at, block):
+        ext[pl.ds(at, LANES), :] = jnp.concatenate([block] * (LANES // ROWS), axis=0).T
+
+    own_in.wait()
+
+    @pl.loop(0, owned // LANES, unroll=8)
+    def _(b):
+        at = pl.multiple_of(b * LANES, LANES)
+        put_rows(at, own_v[:, pl.ds(at, LANES)])
+
+    high_x_in.wait()
+    high_y_in.wait()
+
+    @pl.loop(0, face // LANES, unroll=4)
+    def _(b):
+        at = pl.multiple_of(b * LANES, LANES)
+        got = high_v[0, :, pl.ds(at, LANES)]
+        real, imag = got[: ROWS // 2], got[ROWS // 2 :]
+        turned = jnp.concatenate([cosine * real - sine * imag, sine * real + cosine * imag], axis=0)
+        high_v[0, :, pl.ds(at, LANES)] = turned
+        put_rows(owned + at, turned)
+        put_rows(owned + face + at, high_v[1, :, pl.ds(at, LANES)])
+
+    def idx_row(j, block_id, part):
+        row = j * (capacity // LANES) + block_id * (BLOCK // LANES) + part
+        return jnp.broadcast_to(idx_v[pl.ds(row, 1), :], (LANES // LANE_SETS, LANES))
+
     lane_set = lax.broadcasted_iota(jnp.int32, (1, LANES), 1) >> 4
+    idx_in.wait()
 
     @pl.loop(0, (count + BLOCK - 1) // BLOCK)
     def _(block_id):
@@ -140,13 +275,12 @@
                 inside = range(8 * tile, min(8 * tile + 8, NLOC))
                 row = None
                 for i in inside:
-                    got = ext[pl.ds(idx_s[slot + i * capacity], 1), :]
+                    got = ext[pl.ds(idx_s[i][slot], 1), :]
                     row = got if row is None else jnp.where(lane_set == i % 8, got, row)
                 gathered[tile, pl.ds(e, 1), :] = row
 
         values = jnp.concatenate([gathered[tile] for tile in range(GTILES)], axis=1)
-        pieces = split_bf16(values)
-        products = dot_split(pieces, (kh_ref[...], kl_ref[...]))
+        products = dot_split(split_bf16(values), (kh_ref[...], kl_ref[...]))
         slots = first + lax.broadcasted_iota(jnp.int32, (1, BLOCK), 1)
         live = slots < count
         stiff = jnp.where(live, stiff_ref[:, pl.ds(first, BLOCK)], 0.0)
@@ -155,14 +289,10 @@
         coef = jnp.concatenate(pair * LANE_SETS, axis=0).T
         scaled = [products[:, t * LANES : (t + 1) * LANES] * coef for t in range(TILES)]
 
-        turned = split_bf16(values.T)
-        for t in range(TILES):
-            gram[:, t * LANES : (t + 1) * LANES] += dot_split(turned, split_bf16(scaled[t]))
-
         names = []
         for t in range(TILES):
             rows = [
-                jnp.broadcast_to(idx_v[pl.ds(j * blocks + block_id, 1), :], (LANES // LANE_SETS, BLOCK))
+                jnp.concatenate([idx_row(j, block_id, part) for part in range(BLOCK // LANES)], axis=1)
                 for j in range(LANE_SETS * t, LANE_SETS * t + LANE_SETS)
             ]
             names.append(jnp.concatenate(rows, axis=0).astype(jnp.float32).T)
@@ -172,11 +302,11 @@
                 total = total + jnp.where(names[s] == names[t], scaled[s], 0.0)
             terms[t] = total
 
-        @pl.loop(0, BLOCK, unroll=2)
+        @pl.loop(0, BLOCK, unroll=4)
         def _(e):
             slot = first + e
             added = [terms[t, pl.ds(e, 1), :] for t in range(TILES)]
-            places = [[idx_s[slot + (LANE_SETS * t + g) * capacity] for t in range(TILES)] for g in range(LANE_SETS)]
+            places = [[idx_s[LANE_SETS * t + g][slot] for t in range(TILES)] for g in range(LANE_SETS)]
             held = [[accs[g][pl.ds(places[g][t], 1), :] for t in range(TILES)] for g in range(LANE_SETS)]
             for t in range(TILES):
                 for g in range(LANE_SETS):
@@ -191,36 +321,97 @@
         rows = rows.T
         return (rows[:32] + rows[32:64]) + (rows[64:96] + rows[96:])
 
-    @pl.loop(0, owned // LANES, unroll=4)
+    def wide(at):
+        return jnp.concatenate([summed(at), summed(at + LANES)], axis=1)
+
+    across = (((1,), (1,)), ((), ()))
+    dot = functools.partial(lax.dot_general, dimension_numbers=across, preferred_element_type=jnp.float32)
+
+    def add_gram(left, both):
+        (lh, ll), (bh, bl) = split_bf16(left), split_bf16(both)
+        pieces = dot(jnp.concatenate([lh, ll], axis=0), bh)
+        gram[:, : 2 * ROWS] += pieces[:ROWS] + (pieces[ROWS:] + dot(lh, bl))
+
+    step = 2 * LANES
+
+    @pl.loop(0, face // step, unroll=2)
     def _(b):
-        at = pl.multiple_of(b * LANES, LANES)
-        both = summed(at)
-        curl_out[:, pl.ds(at, LANES)] = both[:ROWS]
-        mass_out[:, pl.ds(at, LANES)] = both[ROWS:]
-
-    @pl.loop(0, face // LANES, unroll=2)
-    def _(b):
-        at = pl.multiple_of(b * LANES, LANES)
-        both = summed(owned + at)
+        at = pl.multiple_of(b * step, step)
+        both = wide(owned + at)
+        add_gram(high_v[0, :, pl.ds(at, step)], both)
+        cos2, sin2 = (jnp.concatenate([row, row], axis=1) for row in (cosine, sine))
         for op in range(2):
             real, imag = both[ROWS * op : ROWS * op + 8], both[ROWS * op + 8 : ROWS * op + ROWS]
-            side_x_out[ROWS * op : ROWS * op + 8, pl.ds(at, LANES)] = cosine * real + sine * imag
-            side_x_out[ROWS * op + 8 : ROWS * op + ROWS, pl.ds(at, LANES)] = cosine * imag - sine * real
-        side_y_out[:, pl.ds(at, LANES)] = summed(owned + face + at)
-
-    total = jnp.zeros((ROWS, LANES), jnp.float32)
-    for j in range(NLOC):
-        t = j // LANE_SETS
-        piece = gram[j * ROWS : (j + 1) * ROWS, t * LANES : (t + 1) * LANES]
-        lanes = lax.broadcasted_iota(jnp.int32, (ROWS, LANES), 1) >> 5
-        total = total + jnp.where(lanes == j % LANE_SETS, piece, 0.0)
-    for shift in (LANES // 2, LANES // 4):
-        total = total + pltpu.roll(total, shift, 1)
+            side_x_out[ROWS * op : ROWS * op + 8, pl.ds(at, step)] = cos2 * real + sin2 * imag
+            side_x_out[ROWS * op + 8 : ROWS * op + ROWS, pl.ds(at, step)] = cos2 * imag - sin2 * real
+        both = wide(owned + face + at)
+        add_gram(high_v[1, :, pl.ds(at, step)], both)
+        side_y_out[:, pl.ds(at, step)] = both
+
+    chunk = owned // OUT_CHUNKS
+
+    def out_copies(c):
+        cols = pl.ds(c * chunk, chunk)
+        return (
+            pltpu.make_async_copy(images.at[pl.ds(0, ROWS), cols], curl_out.at[:, cols], out_sems.at[0, c]),
+            pltpu.make_async_copy(images.at[pl.ds(ROWS, ROWS), cols], mass_out.at[:, cols], out_sems.at[1, c]),
+        )
+
+    for c in range(OUT_CHUNKS):
+
+        @pl.loop(0, chunk // step, unroll=4)
+        def _(b):
+            at = pl.multiple_of(c * chunk + b * step, step)
+            both = wide(at)
+            add_gram(own_v[:, pl.ds(at, step)], both)
+            images[:, pl.ds(at, step)] = both
+
+        for copy in out_copies(c):
+            copy.start()
+
+    total = gram[...]
     of_real, of_imag = total[:8], total[8:]
     odd = ((lax.broadcasted_iota(jnp.int32, (8, LANES), 1) >> 3) & 1) == 1
     gram_out[...] = jnp.where(
         odd, of_real - pltpu.roll(of_imag, 8, 1), of_real + pltpu.roll(of_imag, LANES - 8, 1)
     )
+    for c in range(OUT_CHUNKS):
+        for copy in out_copies(c):
+            copy.wait()
+
+
+def part_images(count, phase, idx, own, high_x, high_y, stiff, mass, kh, kl):
+    shape = jax.ShapeDtypeStruct
+    owned, face = own.shape[1], high_x.shape[1]
+    extent = owned + 2 * face
+    f32 = jnp.float32
+    dma = pltpu.SemaphoreType.DMA
+    return pl.pallas_call(
+        part_kernel,
+        out_shape=(
+            shape((ROWS, owned), f32),
+            shape((ROWS, owned), f32),
+            shape((2 * ROWS, face), f32),
+            shape((2 * ROWS, face), f32),
+            shape((8, LANES), f32),
+        ),
+        in_specs=[SMEM, ANY, ANY, ANY, ANY] + [VMEM] * 6,
+        out_specs=(ANY, ANY, VMEM, VMEM, VMEM),
+        scratch_shapes=[pltpu.VMEM((extent, LANES), f32)] * 5
+        + [
+            pltpu.VMEM((GTILES, BLOCK, LANES), f32),
+            pltpu.VMEM((TILES, BLOCK, LANES), f32),
+            pltpu.VMEM((ROWS, LANES), f32),
+            pltpu.SMEM((idx.size,), jnp.int32),
+            pltpu.VMEM((ROWS, owned), f32),
+            pltpu.VMEM((2, ROWS, face), f32),
+            pltpu.VMEM((2 * ROWS, owned), f32),
+            dma((4,)),
+            dma((2, OUT_CHUNKS)),
+        ],
+        compiler_params=pltpu.CompilerParams(vmem_limit_bytes=VMEM_BYTES),
+        name="part_images",
+    )(count, idx.reshape(-1), own, high_x, high_y, phase, idx, stiff, mass, kh, kl)
 
 
 def exchange_kernel(
@@ -361,54 +552,45 @@
             dma((n_py,)),
         ],
         compiler_params=pltpu.CompilerParams(
-            collective_id=0, has_side_effects=True, vmem_limit_bytes=16 * 2**20
+            collective_id=0, has_side_effects=True, vmem_limit_bytes=VMEM_BYTES
         ),
         name="exchange",
     )(side_x, side_y, gram)
 
 
-def prepare(wraps, dofs, pairing, stiff_mat, mass_mat):
+def finish_kernel(curl_in, mass_in, back_x, back_y, gram_ref, curl_out, mass_out, gram_out, low, sems):
+    face = back_x.shape[1]
+    lows = pl.ds(curl_out.shape[1] - 2 * face, 2 * face)
+    images = (curl_out, mass_out)
+    reads = [pltpu.make_async_copy(images[op].at[:, lows], low.at[op], sems.at[op]) for op in range(2)]
+    writes = [pltpu.make_async_copy(low.at[op], images[op].at[:, lows], sems.at[2 + op]) for op in range(2)]
+    for read in reads:
+        read.start()
+    gram_out[...] = gram_ref[...]
+    for op in range(2):
+        reads[op].wait()
+        low[op, :, :face] += back_x[ROWS * op : ROWS * op + ROWS, :]
+        low[op, :, face:] += back_y[ROWS * op : ROWS * op + ROWS, :]
+        writes[op].start()
+    for write in writes:
+        write.wait()
+
+
+def finish(curl, mass, back_x, back_y, gram):
     shape = jax.ShapeDtypeStruct
-    wide = (GTILES * LANES, TILES * LANES)
     return pl.pallas_call(
-        prepare_kernel,
-        out_shape=(
-            shape(dofs.shape, jnp.int32),
-            shape(wide, jnp.bfloat16),
-            shape(wide, jnp.bfloat16),
-        ),
-        in_specs=[SMEM, VMEM, VMEM, VMEM, VMEM],
-        out_specs=(VMEM, VMEM, VMEM),
-        compiler_params=pltpu.CompilerParams(vmem_limit_bytes=16 * 2**20),
-        name="prepare",
-    )(wraps, dofs, pairing, stiff_mat, mass_mat)
-
-
-def part_images(count, phase, idx, own, high_x, high_y, stiff, mass, kh, kl):
-    shape = jax.ShapeDtypeStruct
-    owned, face = own.shape[1], high_x.shape[1]
-    extent = owned + 2 * face
-    f32 = jnp.float32
-    return pl.pallas_call(
-        part_kernel,
-        out_shape=(
-            shape((ROWS, owned), f32),
-            shape((ROWS, owned), f32),
-            shape((2 * ROWS, face), f32),
-            shape((2 * ROWS, face), f32),
-            shape((8, LANES), f32),
-        ),
-        in_specs=[SMEM, SMEM, SMEM] + [VMEM] * 8,
-        out_specs=(VMEM,) * 5,
-        scratch_shapes=[pltpu.VMEM((extent, LANES), f32)] * 5
-        + [
-            pltpu.VMEM((GTILES, BLOCK, LANES), f32),
-            pltpu.VMEM((TILES, BLOCK, LANES), f32),
-            pltpu.VMEM((GTILES * LANES, TILES * LANES), f32),
+        finish_kernel,
+        out_shape=tuple(shape(value.shape, jnp.float32) for value in (curl, mass, gram)),
+        in_specs=[ANY, ANY, VMEM, VMEM, VMEM],
+        out_specs=(ANY, ANY, VMEM),
+        scratch_shapes=[
+            pltpu.VMEM((2, ROWS, 2 * back_x.shape[1]), jnp.float32),
+            pltpu.SemaphoreType.DMA((4,)),
         ],
-        compiler_params=pltpu.CompilerParams(vmem_limit_bytes=56 * 2**20),
-        name="part_images",
-    )(count, phase, idx.reshape(-1), idx, own, high_x, high_y, stiff, mass, kh, kl)
+        input_output_aliases={0: 0, 1: 1},
+        compiler_params=pltpu.CompilerParams(vmem_limit_bytes=VMEM_BYTES),
+        name="finish",
+    )(curl, mass, back_x, back_y, gram)
 
 
 def on_device(
@@ -423,36 +605,22 @@
     mass_mat,
 ):
     owned = trial_block.shape[-1]
-    face = pairing.shape[0]
-    interior = owned - 2 * face
     own = trial_block.reshape(ROWS, owned)
     n_px, n_py = lax.axis_size("px"), lax.axis_size("py")
-    down_x = [((a + 1) % n_px, a) for a in range(n_px)]
-    down_y = [(b + 1, b) for b in range(n_py - 1)]
-    high_x = lax.ppermute(own[:, interior : interior + face], "px", down_x)
-    high_y = lax.ppermute(own[:, interior + face :], "py", down_y)
-
-    angle = 2.0 * math.pi * bloch_fraction[0].astype(jnp.float32) / bloch_fraction[1].astype(jnp.float32)
-    at_end = lax.axis_index("px") == n_px - 1
-    phase = jnp.stack([jnp.where(at_end, jnp.cos(angle), 1.0), jnp.where(at_end, jnp.sin(angle), 0.0)])
-    wraps = at_end.astype(jnp.int32).reshape(1)
-    idx, kh, kl = prepare(
-        wraps, elem_dofs[0, 0].T.reshape(-1, LANES), pairing.reshape(-1, LANES), stiff_mat, mass_mat
+    high_x, high_y, phase, idx, kh, kl = begin(
+        bloch_fraction,
+        own,
+        elem_dofs[0, 0].T.reshape(-1, LANES),
+        pairing.reshape(-1, LANES),
+        stiff_mat,
+        mass_mat,
     )
     curl, mass, side_x, side_y, gram = part_images(
         elem_count, phase, idx, own, high_x, high_y, stiff_coef[0], mass_coef[0], kh, kl
     )
     back_x, back_y, gram = exchange(side_x, side_y, gram, n_px, n_py)
-
-    def finish(image, add_x, add_y):
-        low_x = image[:, interior : interior + face] + add_x
-        low_y = image[:, interior + face :] + add_y
-        whole = jnp.concatenate([image[:, :interior], low_x, low_y], axis=1)
-        return whole.reshape(trial_block.shape)
-
-    curl = finish(curl, back_x[:ROWS], back_y[:ROWS])
-    mass = finish(mass, back_x[ROWS:], back_y[ROWS:])
-    return curl, mass, gram
+    curl, mass, gram = finish(curl, mass, back_x, back_y, gram)
+    return curl.reshape(trial_block.shape), mass.reshape(trial_block.shape), gram
 
 
 def solution(mesh):

time: 100 us -> 82.2 us (0.82)
  starting transfers between devices: 10.1 us -> 0 us
  local copies, waits for them, and re-layouts: 7.97 us -> 1.56 us
  Pallas kernels: 77.2 us -> 79.1 us
  other arithmetic: 1.75 us -> 0 us
  between operations: 2.95 us -> 1.3 us
    pallas_call x1 -> x2, Pallas kernels: 2.79 us -> 15.8 us  [the longest x1 12.3 us: begin(): pl.pallas_call(begin_kernel, out_shape=(high, high, shape((2, LANES), jnp...]
    ppermute x2 -> x0, starting transfers between devices: 10.1 us -> none  [the longest x1 8.79 us: on_device(): high_x = lax.ppermute(own[:, interior:interior + face], 'px', down_x)]
    pallas_call x1, Pallas kernels: 46 us -> 37.5 us  [exchange(): pl.pallas_call(exchange_kernel, out_shape=(shape(side_x.shape, f32), shap...]
    unnamed x32 -> x1, local copies, waits for them, and re-layouts: 5.3 us -> 0.9 us
    slice x4 -> x0, local copies, waits for them, and re-layouts: 2.65 us -> none  [the longest x2 1.04 us: finish(): whole = jnp.concatenate([image[:, :interior], low_x, low_y], axis=1)]
    pallas_call x1, Pallas kernels: 28.4 us -> 25.8 us  [part_images(): pl.pallas_call(part_kernel, out_shape=(shape((ROWS, owned), f32), shape((...]
    reshape x1 -> x0, other arithmetic: 1.04 us -> none  [finish(): return whole.reshape(trial_block.shape)]
  transfers between devices with their start and end apart: 2 -> 0, of which waited for: 0 -> 0; matrix products, arithmetic and copies ran while one was open for 1% -> 0% of each run, Pallas kernels for 3% -> 0%
where the time goes in v2:
time: 82.2 us; the launch traced here: 81.9 us
  Pallas kernels  79.1 us (96%)
  local copies, waits for them, and re-layouts  1.56 us (2%)
  between operations  1.3 us (2%)
    pallas_call x1, Pallas kernels, exchange(): pl.pallas_call(exchange_kernel, out_shape=(shape(side_x.shape, f32), shap...  37.5 us
    pallas_call x1, Pallas kernels, part_images(): pl.pallas_call(part_kernel, out_shape=(shape((ROWS, owned), f32), shape((...  25.8 us
    pallas_call x1, Pallas kernels, begin(): pl.pallas_call(begin_kernel, out_shape=(high, high, shape((2, LANES), jnp...  12.3 us
    pallas_call x1, Pallas kernels, finish(): pl.pallas_call(finish_kernel, out_shape=tuple((shape(value.shape, jnp.flo...  3.44 us

profile of v2, /device:TPU:1, one launch (start us, length us, event | category | flops | bytes accessed | tf_op | source)
XLA Modules:
  0.0 81.9 jit_solution(9145814551020735760)
XLA Ops:
  1.3 0.9 %copy.16 = s32[1,1,1024,20]{2,3,1,0:T(8,128)S(1)} copy(s32[1,1,1024,20]{2,1,3,0:T(1,128)} %param.13) | data formatting | bytes 163840
  2.2 0.7 reshape.25.dofs_ref
  2.8 12.3 %begin.1 = (f32[16,2048]{1,0:T(8,128)}, f32[16,2048]{1,0:T(8,128)}, f32[2,128]{1,0:T(2,128)}, s32[160,128]{1,0:T(8,128)}, bf16[384,640]{1,0:T(8,128)(2,1)}, /*index=5*/bf16[384,640]{1,0:T(8,128)(2,1)}) custom-call(s32[2]{0:T(128)} %fraction_ref.1, f32[16,8192]{1,0:T(8,128)} %bitcast.12, s32[160,128]{1,0:T(8,128)} %reshape.25.dofs_ref, s32[16,128]{1,0:T(8,128)} %bitcast.18, ...), custom_call_target="tpu_custom_call" | custom-call | tf_op jit(solution)/shard_map/begin/pallas_call | solution.py:162
  15.2 25.8 %part_images.1 = (f32[16,8192]{1,0:T(8,128)}, f32[16,8192]{1,0:T(8,128)}, f32[32,2048]{1,0:T(8,128)}, f32[32,2048]{1,0:T(8,128)}, f32[8,128]{1,0:T(8,128)}) custom-call(s32[1,1]{1,0:T(1,128)S(6)} %copy.19.count_ref, s32[20480]{0:T(1024)} %bitcast.17, f32[16,8192]{1,0:T(8,128)} %bitcast.13, f32[16,2048]{1,0:T(8,128)} %get-tuple-element.21.high_x_hbm, ...), custom_call_target="tpu_custom_call" | custom-call | tf_op jit(solution)/shard_map/part_images/pallas_call | solution.py:389
  41.0 37.5 %exchange.1 = (f32[32,2048]{1,0:T(8,128)}, f32[32,2048]{1,0:T(8,128)}, f32[2,2,8,8]{3,2,1,0:T(8,128)}) custom-call(f32[32,2048]{1,0:T(8,128)} %get-tuple-element.28.side_x_ref, f32[32,2048]{1,0:T(8,128)} %get-tuple-element.29.side_y_ref, f32[8,128]{1,0:T(8,128)} %get-tuple-element.30.gram_ref), custom_call_target="tpu_custom_call" | custom-call | tf_op jit(solution)/shard_map/exchange/pallas_call | solution.py:538
  78.5 3.4 %finish.1 = (f32[16,8192]{1,0:T(8,128)}, f32[16,8192]{1,0:T(8,128)}, f32[2,2,8,8]{3,2,1,0:T(8,128)}) custom-call(f32[16,8192]{1,0:T(8,128)} %get-tuple-element.26.curl_in, f32[16,8192]{1,0:T(8,128)} %get-tuple-element.27.mass_in, f32[32,2048]{1,0:T(8,128)} %get-tuple-element.31.back_x, ...), custom_call_target="tpu_custom_call", output_to_operand_aliasing={{0}: (0, {}), {1}: (1, {})} | custom-call | tf_op jit(solution)/shard_map/finish/pallas_call | solution.py:581

commit v3 on v2

--- a/solution.py
+++ b/solution.py
@@ -23,6 +23,7 @@
 ANY = pl.BlockSpec(memory_space=pl.ANY)
 VMEM_BYTES = 56 * 2**20
 OUT_CHUNKS = 2
+GROUP = 8
 
 
 def split_bf16(value):
@@ -415,182 +416,204 @@
 
 
 def exchange_kernel(
-    side_x_ref,
-    side_y_ref,
+    side_x_hbm,
+    side_y_hbm,
+    curl_hbm,
+    mass_hbm,
     gram_ref,
-    back_x,
-    back_y,
+    lows_out,
     gram_out,
-    along_x,
-    row_sum,
-    along_y,
-    side_send,
-    side_recv,
-    send_x,
-    recv_x,
-    send_y,
-    recv_y,
+    back,
+    low,
+    held,
+    sums,
+    low_sems,
+    side_sems,
+    send_sems,
+    recv_sems,
 ):
-    n_px, n_py = along_x.shape[0], along_y.shape[0]
+    face = side_x_hbm.shape[1]
+    owned = curl_hbm.shape[1]
+    n_px, n_py = lax.axis_size("px"), lax.axis_size("py")
     a, b = lax.axis_index("px"), lax.axis_index("py")
-
+    core, at_y, high = lax.rem(a, 2), lax.rem(a // 2, GROUP), a // (2 * GROUP)
+    at_z, side = lax.rem(b, GROUP), b // GROUP
+
+    def along_y(k):
+        return {"px": high * (2 * GROUP) + k * 2 + core}
+
+    def along_z(k):
+        return {"py": side * GROUP + k}
+
+    def over_rest(k):
+        return {"px": (k // 4) * (2 * GROUP) + at_y * 2 + lax.rem(k, 2), "py": lax.rem(k // 2, 2) * GROUP + at_z}
+
+    groups = ((along_y, at_y), (along_z, at_z), (over_rest, high * 4 + side * 2 + core))
+    next_x, last_x = {"px": lax.rem(a + 1, n_px)}, {"px": lax.rem(a + n_px - 1, n_px)}
+    next_y, last_y = {"py": lax.rem(b + 1, n_py)}, {"py": lax.rem(b + n_py - 1, n_py)}
     barrier = pltpu.get_barrier_semaphore()
 
-    def greet(axis, me, n):
-        @pl.loop(1, n)
-        def _(k):
-            other = lax.rem(me + k, n)
-            pl.semaphore_signal(barrier, 1, device_id={axis: other}, device_id_type=pl.DeviceIdType.MESH)
-
-    greet("px", a, n_px)
-    greet("py", b, n_py)
-    pl.semaphore_wait(barrier, n_px + n_py - 2)
-
-    def tile_copy(axis, to, source, held, at, send, recv):
+    def greet(device):
+        pl.semaphore_signal(barrier, 1, device_id=device, device_id_type=pl.DeviceIdType.MESH)
+
+    for place, me in groups:
+        for k in range(1, GROUP):
+            greet(place(lax.rem(me + k, GROUP)))
+    greet(next_x)
+    greet(last_x)
+
+    @pl.when(b < n_py - 1)
+    def _():
+        greet(next_y)
+
+    @pl.when(b > 0)
+    def _():
+        greet(last_y)
+
+    reads = [
+        pltpu.make_async_copy(image.at[:, pl.ds(owned - 2 * face, 2 * face)], low.at[op], low_sems.at[op])
+        for op, image in enumerate((curl_hbm, mass_hbm))
+    ]
+    write = pltpu.make_async_copy(low, lows_out, low_sems.at[2])
+    for read in reads:
+        read.start()
+    peers = 3 * (GROUP - 1) + 2
+    pl.semaphore_wait(barrier, peers + jnp.minimum(b, 1) + jnp.minimum(n_py - 1 - b, 1))
+
+    def tile_copy(phase, source, to, at):
         return pltpu.make_async_remote_copy(
             src_ref=source,
-            dst_ref=held.at[at],
-            send_sem=send.at[to],
-            recv_sem=recv.at[at],
-            device_id={axis: to},
+            dst_ref=held.at[phase, at],
+            send_sem=send_sems.at[phase, to],
+            recv_sem=recv_sems.at[phase, at],
+            device_id=groups[phase][0](to),
             device_id_type=pl.DeviceIdType.MESH,
         )
 
-    def send_all(axis, me, n, source, held, send, recv):
-        @pl.loop(1, n)
-        def _(k):
-            tile_copy(axis, lax.rem(me + k, n), source, held, me, send, recv).start()
-
-    def sum_all(axis, me, n, source, held, send, recv):
-        held[pl.ds(me, 1)] = source[...][None]
-
-        @pl.loop(1, n)
-        def _(k):
-            other = lax.rem(me + k, n)
-            tile_copy(axis, other, source, held, other, send, recv).wait_recv()
-
-        total = held[0]
-        for at in range(1, n):
-            total = total + held[at]
+    def others(me):
+        return [lax.rem(me + k, GROUP) for k in range(1, GROUP)]
+
+    def send_all(phase, source):
+        me = groups[phase][1]
+        for to in others(me):
+            tile_copy(phase, source, to, me).start()
+        held[phase, pl.ds(me, 1)] = source[...][None]
+
+    def sum_all(phase, source):
+        me = groups[phase][1]
+        for other in others(me):
+            tile_copy(phase, source, other, other).wait_recv()
+        total = held[phase, 0]
+        for at in range(1, GROUP):
+            total = total + held[phase, at]
         return total
 
-    def sent_all(axis, me, n, source, held, send, recv):
-        @pl.loop(1, n)
-        def _(k):
-            tile_copy(axis, lax.rem(me + k, n), source, held, me, send, recv).wait_send()
-
-    def side_copy(source, held, at, axis, to):
+    def side_copy(source, at, device):
         return pltpu.make_async_remote_copy(
             src_ref=source,
-            dst_ref=held,
-            send_sem=side_send.at[at],
-            recv_sem=side_recv.at[at],
-            device_id={axis: to},
+            dst_ref=back.at[at],
+            send_sem=side_sems.at[0, at],
+            recv_sem=side_sems.at[1, at],
+            device_id=device,
             device_id_type=pl.DeviceIdType.MESH,
         )
 
-    over_x = ("px", a, n_px, gram_ref, along_x, send_x, recv_x)
-    over_y = ("py", b, n_py, row_sum, along_y, send_y, recv_y)
-    to_x = side_copy(side_x_ref, back_x, 0, "px", lax.rem(a + 1, n_px))
-    to_y = side_copy(side_y_ref, back_y, 1, "py", lax.rem(b + 1, n_py))
-    send_all(*over_x)
+    to_x = side_copy(side_x_hbm, 0, next_x)
+    to_y = side_copy(side_y_hbm, 1, next_y)
+    send_all(0, gram_ref)
     to_x.start()
 
     @pl.when(b < n_py - 1)
     def _():
         to_y.start()
 
-    row_sum[...] = sum_all(*over_x)
-    send_all(*over_y)
-    whole = sum_all(*over_y)
+    sums[0] = sum_all(0, gram_ref)
+    send_all(1, sums.at[0])
+    for read in reads:
+        read.wait()
+    sums[1] = sum_all(1, sums.at[0])
+    send_all(2, sums.at[1])
+    to_x.wait_recv()
+    for op in range(2):
+        low[op, :, :face] += back[0, ROWS * op : ROWS * op + ROWS, :]
+
+    @pl.when(b > 0)
+    def _():
+        to_y.wait_recv()
+        for op in range(2):
+            low[op, :, face:] += back[1, ROWS * op : ROWS * op + ROWS, :]
+
+    write.start()
+    whole = sum_all(2, sums.at[1])
     for op in range(2):
         for part in range(2):
             at = 16 * op + 8 * part
-            gram_out[op, part] = whole[:, at : at + 8] / gram_scale(n_px, n_py, side_x_ref)
-    to_x.wait_recv()
-
-    @pl.when(b > 0)
-    def _():
-        to_y.wait_recv()
-
-    @pl.when(b == 0)
-    def _():
-        back_y[...] = jnp.zeros_like(back_y)
-
+            gram_out[op, part] = whole[:, at : at + 8] / float(n_px * n_py * owned)
     to_x.wait_send()
 
     @pl.when(b < n_py - 1)
     def _():
         to_y.wait_send()
 
-    sent_all(*over_x)
-    sent_all(*over_y)
-
-
-def gram_scale(n_px, n_py, side_ref):
-    return float(n_px * n_py * 4 * side_ref.shape[1])
-
-
-def exchange(side_x, side_y, gram, n_px, n_py):
+    for phase, source in enumerate((gram_ref, sums.at[0], sums.at[1])):
+        me = groups[phase][1]
+        for to in others(me):
+            tile_copy(phase, source, to, me).wait_send()
+    write.wait()
+
+
+def exchange(side_x, side_y, curl, mass, gram):
     shape = jax.ShapeDtypeStruct
     f32 = jnp.float32
     dma = pltpu.SemaphoreType.DMA
+    face = side_x.shape[1]
     return pl.pallas_call(
         exchange_kernel,
-        out_shape=(shape(side_x.shape, f32), shape(side_y.shape, f32), shape((2, 2, 8, 8), f32)),
-        in_specs=[VMEM] * 3,
-        out_specs=(VMEM,) * 3,
+        out_shape=(shape((2, ROWS, 2 * face), f32), shape((2, 2, 8, 8), f32)),
+        in_specs=[ANY] * 4 + [VMEM],
+        out_specs=(ANY, VMEM),
         scratch_shapes=[
-            pltpu.VMEM((n_px, 8, LANES), f32),
-            pltpu.VMEM((8, LANES), f32),
-            pltpu.VMEM((n_py, 8, LANES), f32),
-            dma((2,)),
-            dma((2,)),
-            dma((n_px,)),
-            dma((n_px,)),
-            dma((n_py,)),
-            dma((n_py,)),
+            pltpu.VMEM((2, 2 * ROWS, face), f32),
+            pltpu.VMEM((2, ROWS, 2 * face), f32),
+            pltpu.VMEM((3, GROUP, 8, LANES), f32),
+            pltpu.VMEM((2, 8, LANES), f32),
+            dma((3,)),
+            dma((2, 2)),
+            dma((3, GROUP)),
+            dma((3, GROUP)),
         ],
         compiler_params=pltpu.CompilerParams(
             collective_id=0, has_side_effects=True, vmem_limit_bytes=VMEM_BYTES
         ),
         name="exchange",
-    )(side_x, side_y, gram)
-
-
-def finish_kernel(curl_in, mass_in, back_x, back_y, gram_ref, curl_out, mass_out, gram_out, low, sems):
-    face = back_x.shape[1]
-    lows = pl.ds(curl_out.shape[1] - 2 * face, 2 * face)
-    images = (curl_out, mass_out)
-    reads = [pltpu.make_async_copy(images[op].at[:, lows], low.at[op], sems.at[op]) for op in range(2)]
-    writes = [pltpu.make_async_copy(low.at[op], images[op].at[:, lows], sems.at[2 + op]) for op in range(2)]
-    for read in reads:
-        read.start()
+    )(side_x, side_y, curl, mass, gram)
+
+
+def finish_kernel(curl_in, mass_in, lows, gram_ref, curl_out, mass_out, gram_out, sems):
+    width = lows.shape[2]
+    writes = [
+        pltpu.make_async_copy(lows.at[op], image.at[:, pl.ds(image.shape[1] - width, width)], sems.at[op])
+        for op, image in enumerate((curl_out, mass_out))
+    ]
+    for write in writes:
+        write.start()
     gram_out[...] = gram_ref[...]
-    for op in range(2):
-        reads[op].wait()
-        low[op, :, :face] += back_x[ROWS * op : ROWS * op + ROWS, :]
-        low[op, :, face:] += back_y[ROWS * op : ROWS * op + ROWS, :]
-        writes[op].start()
     for write in writes:
         write.wait()
 
 
-def finish(curl, mass, back_x, back_y, gram):
+def finish(curl, mass, lows, gram):
     shape = jax.ShapeDtypeStruct
     return pl.pallas_call(
         finish_kernel,
         out_shape=tuple(shape(value.shape, jnp.float32) for value in (curl, mass, gram)),
-        in_specs=[ANY, ANY, VMEM, VMEM, VMEM],
+        in_specs=[ANY, ANY, ANY, VMEM],
         out_specs=(ANY, ANY, VMEM),
-        scratch_shapes=[
-            pltpu.VMEM((2, ROWS, 2 * back_x.shape[1]), jnp.float32),
-            pltpu.SemaphoreType.DMA((4,)),
-        ],
+        scratch_shapes=[pltpu.SemaphoreType.DMA((2,))],
         input_output_aliases={0: 0, 1: 1},
         compiler_params=pltpu.CompilerParams(vmem_limit_bytes=VMEM_BYTES),
         name="finish",
-    )(curl, mass, back_x, back_y, gram)
+    )(curl, mass, lows, gram)
 
 
 def on_device(
@@ -606,7 +629,6 @@
 ):
     owned = trial_block.shape[-1]
     own = trial_block.reshape(ROWS, owned)
-    n_px, n_py = lax.axis_size("px"), lax.axis_size("py")
     high_x, high_y, phase, idx, kh, kl = begin(
         bloch_fraction,
         own,
@@ -618,8 +640,8 @@
     curl, mass, side_x, side_y, gram = part_images(
         elem_count, phase, idx, own, high_x, high_y, stiff_coef[0], mass_coef[0], kh, kl
     )
-    back_x, back_y, gram = exchange(side_x, side_y, gram, n_px, n_py)
-    curl, mass, gram = finish(curl, mass, back_x, back_y, gram)
+    lows, gram = exchange(side_x, side_y, curl, mass, gram)
+    curl, mass, gram = finish(curl, mass, lows, gram)
     return curl.reshape(trial_block.shape), mass.reshape(trial_block.shape), gram
 
 

time: 82.2 us -> 96.8 us (1.18)
  Pallas kernels: 79.1 us -> 93.5 us
    pallas_call x1, Pallas kernels: 3.44 us -> 18.3 us  [finish(): pl.pallas_call(finish_kernel, out_shape=tuple((shape(value.shape, jnp.flo...]
where the time goes in v3:
time: 96.8 us; the launch traced here: 96.4 us
  Pallas kernels  93.5 us (97%)
  local copies, waits for them, and re-layouts  1.56 us (2%)
  between operations  1.3 us (1%)
    pallas_call x1, Pallas kernels, exchange(): pl.pallas_call(exchange_kernel, out_shape=(shape((2, ROWS, 2 * face), f32...  37.1 us
    pallas_call x1, Pallas kernels, part_images(): pl.pallas_call(part_kernel, out_shape=(shape((ROWS, owned), f32), shape((...  25.8 us
    pallas_call x1, Pallas kernels, finish(): pl.pallas_call(finish_kernel, out_shape=tuple((shape(value.shape, jnp.flo...  18.3 us
    pallas_call x1, Pallas kernels, begin(): pl.pallas_call(begin_kernel, out_shape=(high, high, shape((2, LANES), jnp...  12.3 us

profile of v3, /device:TPU:1, one launch (start us, length us, event | category | flops | bytes accessed | tf_op | source)
XLA Modules:
  0.0 96.4 jit_solution(13156062457111136514)
XLA Ops:
  1.3 0.9 copy.16
  2.2 0.7 reshape.25.dofs_ref
  2.8 12.3 %begin.1 = (f32[16,2048]{1,0:T(8,128)}, f32[16,2048]{1,0:T(8,128)}, f32[2,128]{1,0:T(2,128)}, s32[160,128]{1,0:T(8,128)}, bf16[384,640]{1,0:T(8,128)(2,1)}, /*index=5*/bf16[384,640]{1,0:T(8,128)(2,1)}) custom-call(s32[2]{0:T(128)} %fraction_ref.1, f32[16,8192]{1,0:T(8,128)} %bitcast.14, s32[160,128]{1,0:T(8,128)} %reshape.25.dofs_ref, s32[16,128]{1,0:T(8,128)} %bitcast.18, ...), custom_call_target="tpu_custom_call" | custom-call | tf_op jit(solution)/shard_map/begin/pallas_call | solution.py:163
  15.2 25.8 %part_images.1 = (f32[16,8192]{1,0:T(8,128)}, f32[16,8192]{1,0:T(8,128)}, f32[32,2048]{1,0:T(8,128)}, f32[32,2048]{1,0:T(8,128)}, f32[8,128]{1,0:T(8,128)}) custom-call(s32[1,1]{1,0:T(1,128)S(6)} %copy.19.count_ref, s32[20480]{0:T(1024)} %bitcast.17, f32[16,8192]{1,0:T(8,128)} %bitcast.15, f32[16,2048]{1,0:T(8,128)} %get-tuple-element.20.high_x_hbm, ...), custom_call_target="tpu_custom_call" | custom-call | tf_op jit(solution)/shard_map/part_images/pallas_call | solution.py:390
  41.0 37.1 %exchange.1 = (f32[2,16,4096]{2,1,0:T(8,128)}, f32[2,2,8,8]{3,2,1,0:T(8,128)}) custom-call(f32[32,2048]{1,0:T(8,128)} %get-tuple-element.27.side_x_hbm, f32[32,2048]{1,0:T(8,128)} %get-tuple-element.28.side_y_hbm, f32[16,8192]{1,0:T(8,128)} %get-tuple-element.25.curl_hbm.curl_in, f32[16,8192]{1,0:T(8,128)} %get-tuple-element.26.mass_hbm.mass_in, ...), custom_call_target="tpu_custom_call" | custom-call | tf_op jit(solution)/shard_map/exchange/pallas_call | solution.py:570
  78.1 18.3 %finish.1 = (f32[16,8192]{1,0:T(8,128)}, f32[16,8192]{1,0:T(8,128)}, f32[2,2,8,8]{3,2,1,0:T(8,128)}) custom-call(f32[16,8192]{1,0:T(8,128)} %get-tuple-element.25.curl_hbm.curl_in, f32[16,8192]{1,0:T(8,128)} %get-tuple-element.26.mass_hbm.mass_in, f32[2,16,4096]{2,1,0:T(8,128)} %get-tuple-element.30.lows, ...), custom_call_target="tpu_custom_call", output_to_operand_aliasing={{0}: (0, {}), {1}: (1, {})} | custom-call | tf_op jit(solution)/shard_map/finish/pallas_call | solution.py:607

commit v4 on v3

--- a/solution.py
+++ b/solution.py
@@ -42,22 +42,28 @@
 
 def begin_kernel(
     fraction_ref,
-    own_hbm,
+    idx_hbm,
+    own_ref,
     dofs_ref,
     pairing_ref,
     stiff_ref,
     mass_ref,
-    high_x,
-    high_y,
     phase_out,
     idx_out,
     kh_out,
     kl_out,
-    zeros,
+    high_out,
+    gathered,
+    ext,
+    idx_all,
+    head_v,
+    head_s,
+    high_in,
     sems,
 ):
     face = pairing_ref.shape[0] * LANES
-    owned = own_hbm.shape[1]
+    owned = own_ref.shape[1]
+    capacity = idx_all.shape[0] // NLOC
     n_px, n_py = lax.axis_size("px"), lax.axis_size("py")
     a, b = lax.axis_index("px"), lax.axis_index("py")
     below_x, above_x = lax.rem(a + n_px - 1, n_px), lax.rem(a + 1, n_px)
@@ -79,38 +85,29 @@
     def _():
         greet("py", above_y)
 
-    pl.semaphore_wait(barrier, 2 + jnp.minimum(b, 1) + jnp.minimum(n_py - 1 - b, 1))
-
-    def face_copy(first, target, at, axis, to):
+    def face_copy(first, at, axis, to):
         return pltpu.make_async_remote_copy(
-            src_ref=own_hbm.at[:, pl.ds(first, face)],
-            dst_ref=target,
+            src_ref=own_ref.at[:, pl.ds(first, face)],
+            dst_ref=high_in.at[at],
             send_sem=sems.at[2 * at],
             recv_sem=sems.at[2 * at + 1],
             device_id={axis: to},
             device_id_type=pl.DeviceIdType.MESH,
         )
 
-    to_x = face_copy(owned - 2 * face, high_x, 0, "px", below_x)
-    to_y = face_copy(owned - face, high_y, 1, "py", below_y)
-    no_y = pltpu.make_async_copy(zeros, high_y, sems.at[4])
-    to_x.start()
-
-    @pl.when(b > 0)
-    def _():
-        to_y.start()
-
-    @pl.when(b == n_py - 1)
-    def _():
-        zeros[...] = jnp.zeros_like(zeros)
-        no_y.start()
+    to_x = face_copy(owned - 2 * face, 0, "px", below_x)
+    to_y = face_copy(owned - face, 1, "py", below_y)
+    idx_in = pltpu.make_async_copy(idx_hbm, idx_all, sems.at[4])
+    idx_in.start()
 
     at_end = jnp.broadcast_to(a, (1, LANES)) == n_px - 1
     above = jnp.broadcast_to(fraction_ref[0], (1, LANES)).astype(jnp.float32)
     below = jnp.broadcast_to(fraction_ref[1], (1, LANES)).astype(jnp.float32)
     angle = 2.0 * math.pi * above / below
-    phase_out[0:1, :] = jnp.where(at_end, jnp.cos(angle), 1.0)
-    phase_out[1:2, :] = jnp.where(at_end, jnp.sin(angle), 0.0)
+    cosine = jnp.where(at_end, jnp.cos(angle), 1.0)
+    sine = jnp.where(at_end, jnp.sin(angle), 0.0)
+    phase_out[0:1, :] = cosine
+    phase_out[1:2, :] = sine
 
     blocks = dofs_ref.shape[0] // NLOC
     idx_out[...] = dofs_ref[...]
@@ -124,7 +121,12 @@
         here = jnp.take_along_axis(values, local, axis=1)
         found = jnp.where((spot >> 7) == row, here + owned, found)
     wraps = (spot >= 0) & (spot < face) & (jnp.broadcast_to(a, head.shape) == n_px - 1)
-    idx_out[heads, :] = jnp.where(wraps, found, head)
+    head = jnp.where(wraps, found, head)
+    idx_out[heads, :] = head
+    head_v[:NLOC, :] = head
+    head_v[NLOC:, :] = jnp.zeros_like(head_v[NLOC:, :])
+    head_in = pltpu.make_async_copy(head_v, head_s, sems.at[5])
+    head_in.start()
 
     grow = lax.broadcasted_iota(jnp.int32, (GTILES * LANES, NLOC), 0)
     gcol = lax.broadcasted_iota(jnp.int32, (GTILES * LANES, NLOC), 1)
@@ -141,6 +143,43 @@
     both = jnp.where((krow & 15) == (kcol & 15), both, 0.0)
     kh_out[...], kl_out[...] = split_bf16(both)
 
+    def put_rows(at, block):
+        ext[pl.ds(at, LANES), :] = jnp.concatenate([block] * (LANES // ROWS), axis=0).T
+
+    @pl.loop(0, owned // LANES, unroll=8)
+    def _(block):
+        at = pl.multiple_of(block * LANES, LANES)
+        put_rows(at, own_ref[:, pl.ds(at, LANES)])
+
+    lane_set = lax.broadcasted_iota(jnp.int32, (1, LANES), 1) >> 4
+
+    def gather(slot, index):
+        for tile in range(GTILES):
+            row = None
+            for i in range(8 * tile, min(8 * tile + 8, NLOC)):
+                got = ext[pl.ds(index(i, slot), 1), :]
+                row = got if row is None else jnp.where(lane_set == i % 8, got, row)
+            gathered[tile, pl.ds(slot, 1), :] = row
+
+    idx_s = [idx_all.at[pl.ds(j * capacity, capacity)] for j in range(NLOC)]
+    idx_in.wait()
+
+    def gather_slots(first, last):
+        @pl.loop(first, last, unroll=4)
+        def _(slot):
+            gather(slot, lambda i, slot: idx_s[i][slot])
+
+    middle = HALO_SLOTS + (capacity - HALO_SLOTS) // 2
+    gather_slots(HALO_SLOTS, middle)
+
+    pl.semaphore_wait(barrier, 2 + jnp.minimum(b, 1) + jnp.minimum(n_py - 1 - b, 1))
+    to_x.start()
+
+    @pl.when(b > 0)
+    def _():
+        to_y.start()
+
+    gather_slots(middle, capacity)
     to_x.wait()
 
     @pl.when(b > 0)
@@ -153,35 +192,65 @@
 
     @pl.when(b == n_py - 1)
     def _():
-        no_y.wait()
+        high_in[1] = jnp.zeros_like(high_in[1])
+
+    @pl.loop(0, face // LANES, unroll=4)
+    def _(block):
+        at = pl.multiple_of(block * LANES, LANES)
+        got = high_in[0, :, pl.ds(at, LANES)]
+        real, imag = got[: ROWS // 2], got[ROWS // 2 :]
+        turned = jnp.concatenate([cosine * real - sine * imag, sine * real + cosine * imag], axis=0)
+        along_y = high_in[1, :, pl.ds(at, LANES)]
+        high_out[0, :, pl.ds(at, LANES)] = turned
+        high_out[1, :, pl.ds(at, LANES)] = along_y
+        put_rows(owned + at, turned)
+        put_rows(owned + face + at, along_y)
+
+    head_in.wait()
+
+    @pl.loop(0, HALO_SLOTS, unroll=4)
+    def _(slot):
+        gather(slot, lambda i, slot: head_s[i, slot])
 
 
 def begin(fraction, own, dofs, pairing, stiff_mat, mass_mat):
     shape = jax.ShapeDtypeStruct
-    high = shape((ROWS, pairing.size), jnp.float32)
+    f32 = jnp.float32
+    face, owned = pairing.size, own.shape[1]
     spread = shape((GTILES * LANES, TILES * LANES), jnp.bfloat16)
     return pl.pallas_call(
         begin_kernel,
-        out_shape=(high, high, shape((2, LANES), jnp.float32), shape(dofs.shape, jnp.int32), spread, spread),
-        in_specs=[SMEM, ANY, VMEM, VMEM, VMEM, VMEM],
-        out_specs=(ANY, ANY, VMEM, VMEM, VMEM, VMEM),
+        out_shape=(
+            shape((2, LANES), f32),
+            shape(dofs.shape, jnp.int32),
+            spread,
+            spread,
+            shape((2, ROWS, face), f32),
+            shape((GTILES, dofs.size // NLOC, LANES), f32),
+        ),
+        in_specs=[SMEM, ANY] + [VMEM] * 5,
+        out_specs=(VMEM,) * 6,
         scratch_shapes=[
-            pltpu.VMEM(high.shape, jnp.float32),
-            pltpu.SemaphoreType.DMA((5,)),
+            pltpu.VMEM((owned + 2 * face, LANES), f32),
+            pltpu.SMEM((dofs.size,), jnp.int32),
+            pltpu.VMEM((24, LANES), jnp.int32),
+            pltpu.SMEM((24, LANES), jnp.int32),
+            pltpu.VMEM((2, ROWS, face), f32),
+            pltpu.SemaphoreType.DMA((6,)),
         ],
         compiler_params=pltpu.CompilerParams(
             collective_id=1, has_side_effects=True, vmem_limit_bytes=VMEM_BYTES
         ),
         name="begin",
-    )(fraction, own, dofs, pairing, stiff_mat, mass_mat)
+    )(fraction, dofs.reshape(-1), own, dofs, pairing, stiff_mat, mass_mat)
 
 
 def part_kernel(
     count_ref,
     idx_hbm,
     own_hbm,
-    high_x_hbm,
-    high_y_hbm,
+    high_hbm,
+    gathered_hbm,
     phase_ref,
     idx_v,
     stiff_ref,
@@ -193,7 +262,6 @@
     side_x_out,
     side_y_out,
     gram_out,
-    ext,
     acc0,
     acc1,
     acc2,
@@ -217,17 +285,17 @@
     idx_s = [idx_all.at[pl.ds(j * capacity, capacity)] for j in range(NLOC)]
 
     own_in = pltpu.make_async_copy(own_hbm, own_v, in_sems.at[0])
-    high_x_in = pltpu.make_async_copy(high_x_hbm, high_v.at[0], in_sems.at[1])
-    high_y_in = pltpu.make_async_copy(high_y_hbm, high_v.at[1], in_sems.at[2])
+    high_in = pltpu.make_async_copy(high_hbm, high_v, in_sems.at[1])
+    gathered_in = pltpu.make_async_copy(gathered_hbm, gathered, in_sems.at[2])
     idx_in = pltpu.make_async_copy(idx_hbm, idx_all, in_sems.at[3])
+    gathered_in.start()
+    idx_in.start()
     own_in.start()
-    idx_in.start()
-    high_x_in.start()
-    high_y_in.start()
+    high_in.start()
 
     zero_rows = jnp.zeros((LANES, LANES), jnp.float32)
 
-    @pl.loop(0, ext.shape[0] // LANES)
+    @pl.loop(0, acc0.shape[0] // LANES)
     def _(b):
         at = pl.multiple_of(b * LANES, LANES)
         for acc in accs:
@@ -235,52 +303,18 @@
 
     gram[...] = jnp.zeros_like(gram)
 
-    def put_rows(at, block):
-        ext[pl.ds(at, LANES), :] = jnp.concatenate([block] * (LANES // ROWS), axis=0).T
-
-    own_in.wait()
-
-    @pl.loop(0, owned // LANES, unroll=8)
-    def _(b):
-        at = pl.multiple_of(b * LANES, LANES)
-        put_rows(at, own_v[:, pl.ds(at, LANES)])
-
-    high_x_in.wait()
-    high_y_in.wait()
-
-    @pl.loop(0, face // LANES, unroll=4)
-    def _(b):
-        at = pl.multiple_of(b * LANES, LANES)
-        got = high_v[0, :, pl.ds(at, LANES)]
-        real, imag = got[: ROWS // 2], got[ROWS // 2 :]
-        turned = jnp.concatenate([cosine * real - sine * imag, sine * real + cosine * imag], axis=0)
-        high_v[0, :, pl.ds(at, LANES)] = turned
-        put_rows(owned + at, turned)
-        put_rows(owned + face + at, high_v[1, :, pl.ds(at, LANES)])
-
     def idx_row(j, block_id, part):
         row = j * (capacity // LANES) + block_id * (BLOCK // LANES) + part
         return jnp.broadcast_to(idx_v[pl.ds(row, 1), :], (LANES // LANE_SETS, LANES))
 
-    lane_set = lax.broadcasted_iota(jnp.int32, (1, LANES), 1) >> 4
+    gathered_in.wait()
     idx_in.wait()
 
     @pl.loop(0, (count + BLOCK - 1) // BLOCK)
     def _(block_id):
         first = pl.multiple_of(block_id * BLOCK, BLOCK)
 
-        @pl.loop(0, BLOCK, unroll=4)
-        def _(e):
-            slot = first + e
-            for tile in range(GTILES):
-                inside = range(8 * tile, min(8 * tile + 8, NLOC))
-                row = None
-                for i in inside:
-                    got = ext[pl.ds(idx_s[i][slot], 1), :]
-                    row = got if row is None else jnp.where(lane_set == i % 8, got, row)
-                gathered[tile, pl.ds(e, 1), :] = row
-
-        values = jnp.concatenate([gathered[tile] for tile in range(GTILES)], axis=1)
+        values = jnp.concatenate([gathered[tile, pl.ds(first, BLOCK), :] for tile in range(GTILES)], axis=1)
         products = dot_split(split_bf16(values), (kh_ref[...], kl_ref[...]))
         slots = first + lax.broadcasted_iota(jnp.int32, (1, BLOCK), 1)
         live = slots < count
@@ -313,6 +347,8 @@
                 for g in range(LANE_SETS):
                     accs[g][pl.ds(places[g][t], 1), :] = held[g][t] + added[t]
 
+    own_in.wait()
+    high_in.wait()
     quarter = lax.broadcasted_iota(jnp.int32, (LANES, LANES), 1) >> 5
 
     def summed(at):
@@ -381,9 +417,9 @@
             copy.wait()
 
 
-def part_images(count, phase, idx, own, high_x, high_y, stiff, mass, kh, kl):
+def part_images(count, phase, idx, own, high, gathered, stiff, mass, kh, kl):
     shape = jax.ShapeDtypeStruct
-    owned, face = own.shape[1], high_x.shape[1]
+    owned, face = own.shape[1], high.shape[2]
     extent = owned + 2 * face
     f32 = jnp.float32
     dma = pltpu.SemaphoreType.DMA
@@ -398,9 +434,9 @@
         ),
         in_specs=[SMEM, ANY, ANY, ANY, ANY] + [VMEM] * 6,
         out_specs=(ANY, ANY, VMEM, VMEM, VMEM),
-        scratch_shapes=[pltpu.VMEM((extent, LANES), f32)] * 5
+        scratch_shapes=[pltpu.VMEM((extent, LANES), f32)] * 4
         + [
-            pltpu.VMEM((GTILES, BLOCK, LANES), f32),
+            pltpu.VMEM(gathered.shape, f32),
             pltpu.VMEM((TILES, BLOCK, LANES), f32),
             pltpu.VMEM((ROWS, LANES), f32),
             pltpu.SMEM((idx.size,), jnp.int32),
@@ -412,7 +448,7 @@
         ],
         compiler_params=pltpu.CompilerParams(vmem_limit_bytes=VMEM_BYTES),
         name="part_images",
-    )(count, idx.reshape(-1), own, high_x, high_y, phase, idx, stiff, mass, kh, kl)
+    )(count, idx.reshape(-1), own, high, gathered, phase, idx, stiff, mass, kh, kl)
 
 
 def exchange_kernel(
@@ -607,7 +643,7 @@
     return pl.pallas_call(
         finish_kernel,
         out_shape=tuple(shape(value.shape, jnp.float32) for value in (curl, mass, gram)),
-        in_specs=[ANY, ANY, ANY, VMEM],
+        in_specs=[ANY, ANY, VMEM, VMEM],
         out_specs=(ANY, ANY, VMEM),
         scratch_shapes=[pltpu.SemaphoreType.DMA((2,))],
         input_output_aliases={0: 0, 1: 1},
@@ -629,7 +665,7 @@
 ):
     owned = trial_block.shape[-1]
     own = trial_block.reshape(ROWS, owned)
-    high_x, high_y, phase, idx, kh, kl = begin(
+    phase, idx, kh, kl, high, gathered = begin(
         bloch_fraction,
         own,
         elem_dofs[0, 0].T.reshape(-1, LANES),
@@ -638,7 +674,7 @@
         mass_mat,
     )
     curl, mass, side_x, side_y, gram = part_images(
-        elem_count, phase, idx, own, high_x, high_y, stiff_coef[0], mass_coef[0], kh, kl
+        elem_count, phase, idx, own, high, gathered, stiff_coef[0], mass_coef[0], kh, kl
     )
     lows, gram = exchange(side_x, side_y, curl, mass, gram)
     curl, mass, gram = finish(curl, mass, lows, gram)

time: 96.8 us -> 77.4 us (0.80)
  Pallas kernels: 93.5 us -> 73.5 us
    pallas_call x1, Pallas kernels: 18.3 us -> 2.46 us  [finish(): pl.pallas_call(finish_kernel, out_shape=tuple((shape(value.shape, jnp.flo...]
    pallas_call x1, Pallas kernels: 12.3 us -> 23.2 us  [begin(): pl.pallas_call(begin_kernel, out_shape=(shape((2, LANES), f32), shape(dof...]
    pallas_call x1, Pallas kernels: 25.8 us -> 17.7 us  [part_images(): pl.pallas_call(part_kernel, out_shape=(shape((ROWS, owned), f32), shape((...]
    pallas_call x1, Pallas kernels: 37.1 us -> 30.2 us  [exchange(): pl.pallas_call(exchange_kernel, out_shape=(shape((2, ROWS, 2 * face), f32...]
where the time goes in v4:
time: 77.4 us; the launch traced here: 77 us
  Pallas kernels  73.5 us (95%)
  local copies, waits for them, and re-layouts  2.21 us (3%)
  between operations  1.3 us (2%)
    pallas_call x1, Pallas kernels, exchange(): pl.pallas_call(exchange_kernel, out_shape=(shape((2, ROWS, 2 * face), f32...  30.2 us
    pallas_call x1, Pallas kernels, begin(): pl.pallas_call(begin_kernel, out_shape=(shape((2, LANES), f32), shape(dof...  23.2 us
    pallas_call x1, Pallas kernels, part_images(): pl.pallas_call(part_kernel, out_shape=(shape((ROWS, owned), f32), shape((...  17.7 us
    pallas_call x1, Pallas kernels, finish(): pl.pallas_call(finish_kernel, out_shape=tuple((shape(value.shape, jnp.flo...  2.46 us

profile of v4, /device:TPU:1, one launch (start us, length us, event | category | flops | bytes accessed | tf_op | source)
XLA Modules:
  0.0 77.0 jit_solution(15876620907099323145)
XLA Ops:
  1.3 0.9 %copy.16 = s32[1,1,1024,20]{2,3,1,0:T(8,128)S(1)} copy(s32[1,1,1024,20]{2,1,3,0:T(1,128)} %param.13) | data formatting | bytes 163840
  2.2 0.7 reshape.25.dofs_ref
  2.8 0.7 reshape_reshape.3.idx_hbm
  3.5 23.2 %begin.1 = (f32[2,128]{1,0:T(2,128)}, s32[160,128]{1,0:T(8,128)}, bf16[384,640]{1,0:T(8,128)(2,1)}, bf16[384,640]{1,0:T(8,128)(2,1)}, f32[2,16,2048]{2,1,0:T(8,128)}, /*index=5*/f32[3,1024,128]{2,1,0:T(8,128)}) custom-call(s32[2]{0:T(128)} %fraction_ref.1, s32[20480]{0:T(1024)} %reshape_reshape.3.idx_hbm, f32[16,8192]{1,0:T(8,128)} %bitcast.14, ...), custom_call_target="tpu_custom_call" | custom-call | tf_op jit(solution)/shard_map/begin/pallas_call | solution.py:221
  26.7 17.7 %part_images.1 = (f32[16,8192]{1,0:T(8,128)}, f32[16,8192]{1,0:T(8,128)}, f32[32,2048]{1,0:T(8,128)}, f32[32,2048]{1,0:T(8,128)}, f32[8,128]{1,0:T(8,128)}) custom-call(s32[1,1]{1,0:T(1,128)S(6)} %copy.19.count_ref, s32[20480]{0:T(1024)} %bitcast.18, f32[16,8192]{1,0:T(8,128)} %bitcast.15, f32[2,16,2048]{2,1,0:T(8,128)} %get-tuple-element.20.high_hbm, ...), custom_call_target="tpu_custom_call" | custom-call | tf_op jit(solution)/shard_map/part_images/pallas_call | solution.py:426
  44.4 30.2 %exchange.1 = (f32[2,16,4096]{2,1,0:T(8,128)}, f32[2,2,8,8]{3,2,1,0:T(8,128)}) custom-call(f32[32,2048]{1,0:T(8,128)} %get-tuple-element.27.side_x_hbm, f32[32,2048]{1,0:T(8,128)} %get-tuple-element.28.side_y_hbm, f32[16,8192]{1,0:T(8,128)} %get-tuple-element.25.curl_hbm.curl_in, f32[16,8192]{1,0:T(8,128)} %get-tuple-element.26.mass_hbm.mass_in, ...), custom_call_target="tpu_custom_call" | custom-call | tf_op jit(solution)/shard_map/exchange/pallas_call | solution.py:606
  74.6 2.5 %finish.1 = (f32[16,8192]{1,0:T(8,128)}, f32[16,8192]{1,0:T(8,128)}, f32[2,2,8,8]{3,2,1,0:T(8,128)}) custom-call(f32[16,8192]{1,0:T(8,128)} %get-tuple-element.25.curl_hbm.curl_in, f32[16,8192]{1,0:T(8,128)} %get-tuple-element.26.mass_hbm.mass_in, f32[2,16,4096]{2,1,0:T(8,128)} %get-tuple-element.30.lows, ...), custom_call_target="tpu_custom_call", output_to_operand_aliasing={{0}: (0, {}), {1}: (1, {})} | custom-call | tf_op jit(solution)/shard_map/finish/pallas_call | solution.py:643

commit v5 on v3

--- a/solution.py
+++ b/solution.py
@@ -13,7 +13,7 @@
 ROWS = 16
 NLOC = 20
 HALO_SLOTS = 128
-BLOCK = 256
+BLOCK = 512
 TILES = 5
 GTILES = 3
 LANE_SETS = 4
@@ -112,10 +112,13 @@
     phase_out[0:1, :] = jnp.where(at_end, jnp.cos(angle), 1.0)
     phase_out[1:2, :] = jnp.where(at_end, jnp.sin(angle), 0.0)
 
-    blocks = dofs_ref.shape[0] // NLOC
-    idx_out[...] = dofs_ref[...]
+    blocks = idx_out.shape[0] // NLOC
+    for j in range(NLOC):
+        for block in range(blocks):
+            row = j * blocks + block
+            idx_out[row : row + 1, :] = dofs_ref[j, :, block * LANES : (block + 1) * LANES]
     heads = pl.ds(0, NLOC, stride=blocks)
-    head = dofs_ref[heads, :]
+    head = idx_out[heads, :]
     spot = head - owned
     local = spot & (LANES - 1)
     found = jnp.zeros_like(head)
@@ -162,7 +165,7 @@
     spread = shape((GTILES * LANES, TILES * LANES), jnp.bfloat16)
     return pl.pallas_call(
         begin_kernel,
-        out_shape=(high, high, shape((2, LANES), jnp.float32), shape(dofs.shape, jnp.int32), spread, spread),
+        out_shape=(high, high, shape((2, LANES), jnp.float32), shape((dofs.size // LANES, LANES), jnp.int32), spread, spread),
         in_specs=[SMEM, ANY, VMEM, VMEM, VMEM, VMEM],
         out_specs=(ANY, ANY, VMEM, VMEM, VMEM, VMEM),
         scratch_shapes=[
@@ -186,12 +189,12 @@
     idx_v,
     stiff_ref,
     mass_ref,
-    kh_ref,
-    kl_ref,
+    kh_hbm,
+    kl_hbm,
     curl_out,
     mass_out,
-    side_x_out,
-    side_y_out,
+    side_x_hbm,
+    side_y_hbm,
     gram_out,
     ext,
     acc0,
@@ -205,6 +208,10 @@
     own_v,
     high_v,
     images,
+    kh_ref,
+    kl_ref,
+    side_x_out,
+    side_y_out,
     in_sems,
     out_sems,
 ):
@@ -224,6 +231,10 @@
     idx_in.start()
     high_x_in.start()
     high_y_in.start()
+    kh_in = pltpu.make_async_copy(kh_hbm, kh_ref, in_sems.at[4])
+    kl_in = pltpu.make_async_copy(kl_hbm, kl_ref, in_sems.at[5])
+    kh_in.start()
+    kl_in.start()
 
     zero_rows = jnp.zeros((LANES, LANES), jnp.float32)
 
@@ -264,6 +275,8 @@
 
     lane_set = lax.broadcasted_iota(jnp.int32, (1, LANES), 1) >> 4
     idx_in.wait()
+    kh_in.wait()
+    kl_in.wait()
 
     @pl.loop(0, (count + BLOCK - 1) // BLOCK)
     def _(block_id):
@@ -303,7 +316,7 @@
                 total = total + jnp.where(names[s] == names[t], scaled[s], 0.0)
             terms[t] = total
 
-        @pl.loop(0, BLOCK, unroll=4)
+        @pl.loop(0, BLOCK, unroll=8)
         def _(e):
             slot = first + e
             added = [terms[t, pl.ds(e, 1), :] for t in range(TILES)]
@@ -349,6 +362,10 @@
         add_gram(high_v[1, :, pl.ds(at, step)], both)
         side_y_out[:, pl.ds(at, step)] = both
 
+    side_x_put = pltpu.make_async_copy(side_x_out, side_x_hbm, in_sems.at[6])
+    side_y_put = pltpu.make_async_copy(side_y_out, side_y_hbm, in_sems.at[7])
+    side_x_put.start()
+    side_y_put.start()
     chunk = owned // OUT_CHUNKS
 
     def out_copies(c):
@@ -360,7 +377,7 @@
 
     for c in range(OUT_CHUNKS):
 
-        @pl.loop(0, chunk // step, unroll=4)
+        @pl.loop(0, chunk // step, unroll=8)
         def _(b):
             at = pl.multiple_of(c * chunk + b * step, step)
             both = wide(at)
@@ -376,6 +393,8 @@
     gram_out[...] = jnp.where(
         odd, of_real - pltpu.roll(of_imag, 8, 1), of_real + pltpu.roll(of_imag, LANES - 8, 1)
     )
+    side_x_put.wait()
+    side_y_put.wait()
     for c in range(OUT_CHUNKS):
         for copy in out_copies(c):
             copy.wait()
@@ -396,8 +415,8 @@
             shape((2 * ROWS, face), f32),
             shape((8, LANES), f32),
         ),
-        in_specs=[SMEM, ANY, ANY, ANY, ANY] + [VMEM] * 6,
-        out_specs=(ANY, ANY, VMEM, VMEM, VMEM),
+        in_specs=[SMEM, ANY, ANY, ANY, ANY] + [VMEM] * 4 + [ANY] * 2,
+        out_specs=(ANY, ANY, ANY, ANY, VMEM),
         scratch_shapes=[pltpu.VMEM((extent, LANES), f32)] * 5
         + [
             pltpu.VMEM((GTILES, BLOCK, LANES), f32),
@@ -407,7 +426,11 @@
             pltpu.VMEM((ROWS, owned), f32),
             pltpu.VMEM((2, ROWS, face), f32),
             pltpu.VMEM((2 * ROWS, owned), f32),
-            dma((4,)),
+            pltpu.VMEM(kh.shape, kh.dtype),
+            pltpu.VMEM(kl.shape, kl.dtype),
+            pltpu.VMEM((2 * ROWS, face), f32),
+            pltpu.VMEM((2 * ROWS, face), f32),
+            dma((8,)),
             dma((2, OUT_CHUNKS)),
         ],
         compiler_params=pltpu.CompilerParams(vmem_limit_bytes=VMEM_BYTES),
@@ -420,12 +443,13 @@
     side_y_hbm,
     curl_hbm,
     mass_hbm,
-    gram_ref,
+    gram_hbm,
     lows_out,
     gram_out,
     back,
     low,
     held,
+    gram_ref,
     sums,
     low_sems,
     side_sems,
@@ -451,6 +475,8 @@
     groups = ((along_y, at_y), (along_z, at_z), (over_rest, high * 4 + side * 2 + core))
     next_x, last_x = {"px": lax.rem(a + 1, n_px)}, {"px": lax.rem(a + n_px - 1, n_px)}
     next_y, last_y = {"py": lax.rem(b + 1, n_py)}, {"py": lax.rem(b + n_py - 1, n_py)}
+    gram_in = pltpu.make_async_copy(gram_hbm, gram_ref, low_sems.at[3])
+    gram_in.start()
     barrier = pltpu.get_barrier_semaphore()
 
     def greet(device):
@@ -477,6 +503,7 @@
     write = pltpu.make_async_copy(low, lows_out, low_sems.at[2])
     for read in reads:
         read.start()
+    gram_in.wait()
     peers = 3 * (GROUP - 1) + 2
     pl.semaphore_wait(barrier, peers + jnp.minimum(b, 1) + jnp.minimum(n_py - 1 - b, 1))
 
@@ -570,14 +597,15 @@
     return pl.pallas_call(
         exchange_kernel,
         out_shape=(shape((2, ROWS, 2 * face), f32), shape((2, 2, 8, 8), f32)),
-        in_specs=[ANY] * 4 + [VMEM],
+        in_specs=[ANY] * 5,
         out_specs=(ANY, VMEM),
         scratch_shapes=[
             pltpu.VMEM((2, 2 * ROWS, face), f32),
             pltpu.VMEM((2, ROWS, 2 * face), f32),
             pltpu.VMEM((3, GROUP, 8, LANES), f32),
+            pltpu.VMEM((8, LANES), f32),
             pltpu.VMEM((2, 8, LANES), f32),
-            dma((3,)),
+            dma((4,)),
             dma((2, 2)),
             dma((3, GROUP)),
             dma((3, GROUP)),
@@ -607,7 +635,7 @@
     return pl.pallas_call(
         finish_kernel,
         out_shape=tuple(shape(value.shape, jnp.float32) for value in (curl, mass, gram)),
-        in_specs=[ANY, ANY, ANY, VMEM],
+        in_specs=[ANY, ANY, VMEM, VMEM],
         out_specs=(ANY, ANY, VMEM),
         scratch_shapes=[pltpu.SemaphoreType.DMA((2,))],
         input_output_aliases={0: 0, 1: 1},
@@ -632,7 +660,7 @@
     high_x, high_y, phase, idx, kh, kl = begin(
         bloch_fraction,
         own,
-        elem_dofs[0, 0].T.reshape(-1, LANES),
+        elem_dofs[0].transpose(2, 0, 1),
         pairing.reshape(-1, LANES),
         stiff_mat,
         mass_mat,

time: 96.8 us -> 76.9 us (0.79)
  Pallas kernels: 93.5 us -> 75.3 us
  local copies, waits for them, and re-layouts: 1.56 us -> 0 us
    pallas_call x1, Pallas kernels: 18.3 us -> 2.46 us  [finish(): pl.pallas_call(finish_kernel, out_shape=tuple((shape(value.shape, jnp.flo...]
    pallas_call x1, Pallas kernels: 25.8 us -> 23.8 us  [part_images(): pl.pallas_call(part_kernel, out_shape=(shape((ROWS, owned), f32), shape((...]
where the time goes in v5:
time: 76.9 us; the launch traced here: 76.6 us
  Pallas kernels  75.3 us (98%)
  between operations  1.3 us (2%)
    pallas_call x1, Pallas kernels, exchange(): pl.pallas_call(exchange_kernel, out_shape=(shape((2, ROWS, 2 * face), f32...  36.7 us
    pallas_call x1, Pallas kernels, part_images(): pl.pallas_call(part_kernel, out_shape=(shape((ROWS, owned), f32), shape((...  23.8 us
    pallas_call x1, Pallas kernels, begin(): pl.pallas_call(begin_kernel, out_shape=(high, high, shape((2, LANES), jnp...  12.4 us
    pallas_call x1, Pallas kernels, finish(): pl.pallas_call(finish_kernel, out_shape=tuple((shape(value.shape, jnp.flo...  2.46 us

profile of v5, /device:TPU:1, one launch (start us, length us, event | category | flops | bytes accessed | tf_op | source)
XLA Modules:
  0.0 76.6 jit_solution(15536314776020636612)
XLA Ops:
  1.3 12.4 %begin.1 = (f32[16,2048]{1,0:T(8,128)}, f32[16,2048]{1,0:T(8,128)}, f32[2,128]{1,0:T(2,128)}, s32[160,128]{1,0:T(8,128)}, bf16[384,640]{1,0:T(8,128)(2,1)}, /*index=5*/bf16[384,640]{1,0:T(8,128)(2,1)}) custom-call(s32[2]{0:T(128)} %fraction_ref.1, f32[16,8192]{1,0:T(8,128)} %bitcast.12, s32[20,1,1024]{2,1,0:T(1,128)} %bitcast.15, s32[16,128]{1,0:T(8,128)} %bitcast.16, ...), custom_call_target="tpu_custom_call" | custom-call | tf_op jit(solution)/shard_map/begin/pallas_call | solution.py:166
  13.7 23.8 %part_images.1 = (f32[16,8192]{1,0:T(8,128)}, f32[16,8192]{1,0:T(8,128)}, f32[32,2048]{1,0:T(8,128)}, f32[32,2048]{1,0:T(8,128)}, f32[8,128]{1,0:T(8,128)}) custom-call(s32[1,1]{1,0:T(1,128)S(6)} %copy.16.count_ref, s32[20480]{0:T(1024)} %bitcast.14, f32[16,8192]{1,0:T(8,128)} %bitcast.13, f32[16,2048]{1,0:T(8,128)} %get-tuple-element.20.high_x_hbm, ...), custom_call_target="tpu_custom_call" | custom-call | tf_op jit(solution)/shard_map/part_images/pallas_call | solution.py:409
  37.5 36.7 %exchange.1 = (f32[2,16,4096]{2,1,0:T(8,128)}, f32[2,2,8,8]{3,2,1,0:T(8,128)}) custom-call(f32[32,2048]{1,0:T(8,128)} %get-tuple-element.27.side_x_hbm, f32[32,2048]{1,0:T(8,128)} %get-tuple-element.28.side_y_hbm, f32[16,8192]{1,0:T(8,128)} %get-tuple-element.25.curl_hbm.curl_in, f32[16,8192]{1,0:T(8,128)} %get-tuple-element.26.mass_hbm.mass_in, ...), custom_call_target="tpu_custom_call" | custom-call | tf_op jit(solution)/shard_map/exchange/pallas_call | solution.py:597
  74.2 2.5 %finish.1 = (f32[16,8192]{1,0:T(8,128)}, f32[16,8192]{1,0:T(8,128)}, f32[2,2,8,8]{3,2,1,0:T(8,128)}) custom-call(f32[16,8192]{1,0:T(8,128)} %get-tuple-element.25.curl_hbm.curl_in, f32[16,8192]{1,0:T(8,128)} %get-tuple-element.26.mass_hbm.mass_in, f32[2,16,4096]{2,1,0:T(8,128)} %get-tuple-element.30.lows, ...), custom_call_target="tpu_custom_call", output_to_operand_aliasing={{0}: (0, {}), {1}: (1, {})} | custom-call | tf_op jit(solution)/shard_map/finish/pallas_call | solution.py:635

commit v6 on v5

--- a/solution.py
+++ b/solution.py
@@ -238,7 +238,7 @@
 
     zero_rows = jnp.zeros((LANES, LANES), jnp.float32)
 
-    @pl.loop(0, ext.shape[0] // LANES)
+    @pl.loop(0, ext.shape[0] // LANES, unroll=4)
     def _(b):
         at = pl.multiple_of(b * LANES, LANES)
         for acc in accs:
@@ -251,7 +251,7 @@
 
     own_in.wait()
 
-    @pl.loop(0, owned // LANES, unroll=8)
+    @pl.loop(0, owned // LANES, unroll=16)
     def _(b):
         at = pl.multiple_of(b * LANES, LANES)
         put_rows(at, own_v[:, pl.ds(at, LANES)])
@@ -259,7 +259,7 @@
     high_x_in.wait()
     high_y_in.wait()
 
-    @pl.loop(0, face // LANES, unroll=4)
+    @pl.loop(0, face // LANES, unroll=8)
     def _(b):
         at = pl.multiple_of(b * LANES, LANES)
         got = high_v[0, :, pl.ds(at, LANES)]
@@ -316,7 +316,7 @@
                 total = total + jnp.where(names[s] == names[t], scaled[s], 0.0)
             terms[t] = total
 
-        @pl.loop(0, BLOCK, unroll=8)
+        @pl.loop(0, BLOCK, unroll=16)
         def _(e):
             slot = first + e
             added = [terms[t, pl.ds(e, 1), :] for t in range(TILES)]
@@ -348,7 +348,7 @@
 
     step = 2 * LANES
 
-    @pl.loop(0, face // step, unroll=2)
+    @pl.loop(0, face // step, unroll=4)
     def _(b):
         at = pl.multiple_of(b * step, step)
         both = wide(owned + at)
@@ -377,7 +377,7 @@
 
     for c in range(OUT_CHUNKS):
 
-        @pl.loop(0, chunk // step, unroll=8)
+        @pl.loop(0, chunk // step, unroll=16)
         def _(b):
             at = pl.multiple_of(c * chunk + b * step, step)
             both = wide(at)
@@ -472,7 +472,7 @@
     def over_rest(k):
         return {"px": (k // 4) * (2 * GROUP) + at_y * 2 + lax.rem(k, 2), "py": lax.rem(k // 2, 2) * GROUP + at_z}
 
-    groups = ((along_y, at_y), (along_z, at_z), (over_rest, high * 4 + side * 2 + core))
+    groups = ((over_rest, high * 4 + side * 2 + core), (along_y, at_y), (along_z, at_z))
     next_x, last_x = {"px": lax.rem(a + 1, n_px)}, {"px": lax.rem(a + n_px - 1, n_px)}
     next_y, last_y = {"py": lax.rem(b + 1, n_py)}, {"py": lax.rem(b + n_py - 1, n_py)}
     gram_in = pltpu.make_async_copy(gram_hbm, gram_ref, low_sems.at[3])
@@ -617,15 +617,19 @@
     )(side_x, side_y, curl, mass, gram)
 
 
-def finish_kernel(curl_in, mass_in, lows, gram_ref, curl_out, mass_out, gram_out, sems):
+def finish_kernel(curl_in, mass_in, lows_hbm, gram_ref, curl_out, mass_out, gram_out, lows, sems):
     width = lows.shape[2]
+    reads = [pltpu.make_async_copy(lows_hbm.at[op], lows.at[op], sems.at[0, op]) for op in range(2)]
     writes = [
-        pltpu.make_async_copy(lows.at[op], image.at[:, pl.ds(image.shape[1] - width, width)], sems.at[op])
+        pltpu.make_async_copy(lows.at[op], image.at[:, pl.ds(image.shape[1] - width, width)], sems.at[1, op])
         for op, image in enumerate((curl_out, mass_out))
     ]
-    for write in writes:
+    for read in reads:
+        read.start()
+    gram_out[...] = gram_ref[...]
+    for read, write in zip(reads, writes):
+        read.wait()
         write.start()
-    gram_out[...] = gram_ref[...]
     for write in writes:
         write.wait()
 
@@ -635,9 +639,9 @@
     return pl.pallas_call(
         finish_kernel,
         out_shape=tuple(shape(value.shape, jnp.float32) for value in (curl, mass, gram)),
-        in_specs=[ANY, ANY, VMEM, VMEM],
+        in_specs=[ANY, ANY, ANY, VMEM],
         out_specs=(ANY, ANY, VMEM),
-        scratch_shapes=[pltpu.SemaphoreType.DMA((2,))],
+        scratch_shapes=[pltpu.VMEM(lows.shape, jnp.float32), pltpu.SemaphoreType.DMA((2, 2))],
         input_output_aliases={0: 0, 1: 1},
         compiler_params=pltpu.CompilerParams(vmem_limit_bytes=VMEM_BYTES),
         name="finish",

time: 76.9 us -> 75.6 us (0.983)
  Pallas kernels: 75.3 us -> 74 us
    pallas_call x1, Pallas kernels: 23.8 us -> 22.1 us  [part_images(): pl.pallas_call(part_kernel, out_shape=(shape((ROWS, owned), f32), shape((...]
where the time goes in v6:
time: 75.6 us; the launch traced here: 75.3 us
  Pallas kernels  74 us (98%)
  between operations  1.3 us (2%)
    pallas_call x1, Pallas kernels, exchange(): pl.pallas_call(exchange_kernel, out_shape=(shape((2, ROWS, 2 * face), f32...  36.4 us
    pallas_call x1, Pallas kernels, part_images(): pl.pallas_call(part_kernel, out_shape=(shape((ROWS, owned), f32), shape((...  22.1 us
    pallas_call x1, Pallas kernels, begin(): pl.pallas_call(begin_kernel, out_shape=(high, high, shape((2, LANES), jnp...  12.4 us
    pallas_call x1, Pallas kernels, finish(): pl.pallas_call(finish_kernel, out_shape=tuple((shape(value.shape, jnp.flo...  3.1 us

profile of v6, /device:TPU:1, one launch (start us, length us, event | category | flops | bytes accessed | tf_op | source)
XLA Modules:
  0.0 75.3 jit_solution(15038460414631755719)
XLA Ops:
  1.3 12.4 %begin.1 = (f32[16,2048]{1,0:T(8,128)}, f32[16,2048]{1,0:T(8,128)}, f32[2,128]{1,0:T(2,128)}, s32[160,128]{1,0:T(8,128)}, bf16[384,640]{1,0:T(8,128)(2,1)}, /*index=5*/bf16[384,640]{1,0:T(8,128)(2,1)}) custom-call(s32[2]{0:T(128)} %fraction_ref.1, f32[16,8192]{1,0:T(8,128)} %bitcast.12, s32[20,1,1024]{2,1,0:T(1,128)} %bitcast.15, s32[16,128]{1,0:T(8,128)} %bitcast.16, ...), custom_call_target="tpu_custom_call" | custom-call | tf_op jit(solution)/shard_map/begin/pallas_call | solution.py:166
  13.7 22.1 %part_images.1 = (f32[16,8192]{1,0:T(8,128)}, f32[16,8192]{1,0:T(8,128)}, f32[32,2048]{1,0:T(8,128)}, f32[32,2048]{1,0:T(8,128)}, f32[8,128]{1,0:T(8,128)}) custom-call(s32[1,1]{1,0:T(1,128)S(6)} %copy.16.count_ref, s32[20480]{0:T(1024)} %bitcast.14, f32[16,8192]{1,0:T(8,128)} %bitcast.13, f32[16,2048]{1,0:T(8,128)} %get-tuple-element.20.high_x_hbm, ...), custom_call_target="tpu_custom_call" | custom-call | tf_op jit(solution)/shard_map/part_images/pallas_call | solution.py:409
  35.8 36.4 %exchange.1 = (f32[2,16,4096]{2,1,0:T(8,128)}, f32[2,2,8,8]{3,2,1,0:T(8,128)}) custom-call(f32[32,2048]{1,0:T(8,128)} %get-tuple-element.27.side_x_hbm, f32[32,2048]{1,0:T(8,128)} %get-tuple-element.28.side_y_hbm, f32[16,8192]{1,0:T(8,128)} %get-tuple-element.25.curl_hbm.curl_in, f32[16,8192]{1,0:T(8,128)} %get-tuple-element.26.mass_hbm.mass_in, ...), custom_call_target="tpu_custom_call" | custom-call | tf_op jit(solution)/shard_map/exchange/pallas_call | solution.py:597
  72.2 3.1 %finish.1 = (f32[16,8192]{1,0:T(8,128)}, f32[16,8192]{1,0:T(8,128)}, f32[2,2,8,8]{3,2,1,0:T(8,128)}) custom-call(f32[16,8192]{1,0:T(8,128)} %get-tuple-element.25.curl_hbm.curl_in, f32[16,8192]{1,0:T(8,128)} %get-tuple-element.26.mass_hbm.mass_in, f32[2,16,4096]{2,1,0:T(8,128)} %get-tuple-element.30.lows_hbm, ...), custom_call_target="tpu_custom_call", output_to_operand_aliasing={{0}: (0, {}), {1}: (1, {})} | custom-call | tf_op jit(solution)/shard_map/finish/pallas_call | solution.py:639

commit v7 on v5

--- a/solution.py
+++ b/solution.py
@@ -238,7 +238,7 @@
 
     zero_rows = jnp.zeros((LANES, LANES), jnp.float32)
 
-    @pl.loop(0, ext.shape[0] // LANES)
+    @pl.loop(0, ext.shape[0] // LANES, unroll=4)
     def _(b):
         at = pl.multiple_of(b * LANES, LANES)
         for acc in accs:
@@ -251,7 +251,7 @@
 
     own_in.wait()
 
-    @pl.loop(0, owned // LANES, unroll=8)
+    @pl.loop(0, owned // LANES, unroll=16)
     def _(b):
         at = pl.multiple_of(b * LANES, LANES)
         put_rows(at, own_v[:, pl.ds(at, LANES)])
@@ -259,7 +259,7 @@
     high_x_in.wait()
     high_y_in.wait()
 
-    @pl.loop(0, face // LANES, unroll=4)
+    @pl.loop(0, face // LANES, unroll=8)
     def _(b):
         at = pl.multiple_of(b * LANES, LANES)
         got = high_v[0, :, pl.ds(at, LANES)]
@@ -316,7 +316,7 @@
                 total = total + jnp.where(names[s] == names[t], scaled[s], 0.0)
             terms[t] = total
 
-        @pl.loop(0, BLOCK, unroll=8)
+        @pl.loop(0, BLOCK, unroll=16)
         def _(e):
             slot = first + e
             added = [terms[t, pl.ds(e, 1), :] for t in range(TILES)]
@@ -348,7 +348,7 @@
 
     step = 2 * LANES
 
-    @pl.loop(0, face // step, unroll=2)
+    @pl.loop(0, face // step, unroll=4)
     def _(b):
         at = pl.multiple_of(b * step, step)
         both = wide(owned + at)
@@ -377,7 +377,7 @@
 
     for c in range(OUT_CHUNKS):
 
-        @pl.loop(0, chunk // step, unroll=8)
+        @pl.loop(0, chunk // step, unroll=16)
         def _(b):
             at = pl.multiple_of(c * chunk + b * step, step)
             both = wide(at)
@@ -472,7 +472,7 @@
     def over_rest(k):
         return {"px": (k // 4) * (2 * GROUP) + at_y * 2 + lax.rem(k, 2), "py": lax.rem(k // 2, 2) * GROUP + at_z}
 
-    groups = ((along_y, at_y), (along_z, at_z), (over_rest, high * 4 + side * 2 + core))
+    groups = ((over_rest, high * 4 + side * 2 + core), (along_y, at_y), (along_z, at_z))
     next_x, last_x = {"px": lax.rem(a + 1, n_px)}, {"px": lax.rem(a + n_px - 1, n_px)}
     next_y, last_y = {"py": lax.rem(b + 1, n_py)}, {"py": lax.rem(b + n_py - 1, n_py)}
     gram_in = pltpu.make_async_copy(gram_hbm, gram_ref, low_sems.at[3])

time: 76.9 us -> 76.6 us (level)
    pallas_call x1, Pallas kernels: 36.7 us -> 38.5 us  [exchange(): pl.pallas_call(exchange_kernel, out_shape=(shape((2, ROWS, 2 * face), f32...]
    pallas_call x1, Pallas kernels: 23.8 us -> 22.1 us  [part_images(): pl.pallas_call(part_kernel, out_shape=(shape((ROWS, owned), f32), shape((...]
where the time goes in v7:
time: 76.6 us; the launch traced here: 76.8 us
  Pallas kernels  75.5 us (99%)
  between operations  1.3 us (2%)
    pallas_call x1, Pallas kernels, exchange(): pl.pallas_call(exchange_kernel, out_shape=(shape((2, ROWS, 2 * face), f32...  38.5 us
    pallas_call x1, Pallas kernels, part_images(): pl.pallas_call(part_kernel, out_shape=(shape((ROWS, owned), f32), shape((...  22.1 us
    pallas_call x1, Pallas kernels, begin(): pl.pallas_call(begin_kernel, out_shape=(high, high, shape((2, LANES), jnp...  12.4 us
    pallas_call x1, Pallas kernels, finish(): pl.pallas_call(finish_kernel, out_shape=tuple((shape(value.shape, jnp.flo...  2.46 us

profile of v7, /device:TPU:1, one launch (start us, length us, event | category | flops | bytes accessed | tf_op | source)
XLA Modules:
  0.0 76.8 jit_solution(10972026559213492372)
XLA Ops:
  1.3 12.4 %begin.1 = (f32[16,2048]{1,0:T(8,128)}, f32[16,2048]{1,0:T(8,128)}, f32[2,128]{1,0:T(2,128)}, s32[160,128]{1,0:T(8,128)}, bf16[384,640]{1,0:T(8,128)(2,1)}, /*index=5*/bf16[384,640]{1,0:T(8,128)(2,1)}) custom-call(s32[2]{0:T(128)} %fraction_ref.1, f32[16,8192]{1,0:T(8,128)} %bitcast.12, s32[20,1,1024]{2,1,0:T(1,128)} %bitcast.15, s32[16,128]{1,0:T(8,128)} %bitcast.16, ...), custom_call_target="tpu_custom_call" | custom-call | tf_op jit(solution)/shard_map/begin/pallas_call | solution.py:166
  13.7 22.1 %part_images.1 = (f32[16,8192]{1,0:T(8,128)}, f32[16,8192]{1,0:T(8,128)}, f32[32,2048]{1,0:T(8,128)}, f32[32,2048]{1,0:T(8,128)}, f32[8,128]{1,0:T(8,128)}) custom-call(s32[1,1]{1,0:T(1,128)S(6)} %copy.16.count_ref, s32[20480]{0:T(1024)} %bitcast.14, f32[16,8192]{1,0:T(8,128)} %bitcast.13, f32[16,2048]{1,0:T(8,128)} %get-tuple-element.20.high_x_hbm, ...), custom_call_target="tpu_custom_call" | custom-call | tf_op jit(solution)/shard_map/part_images/pallas_call | solution.py:409
  35.8 38.5 %exchange.1 = (f32[2,16,4096]{2,1,0:T(8,128)}, f32[2,2,8,8]{3,2,1,0:T(8,128)}) custom-call(f32[32,2048]{1,0:T(8,128)} %get-tuple-element.27.side_x_hbm, f32[32,2048]{1,0:T(8,128)} %get-tuple-element.28.side_y_hbm, f32[16,8192]{1,0:T(8,128)} %get-tuple-element.25.curl_hbm.curl_in, f32[16,8192]{1,0:T(8,128)} %get-tuple-element.26.mass_hbm.mass_in, ...), custom_call_target="tpu_custom_call" | custom-call | tf_op jit(solution)/shard_map/exchange/pallas_call | solution.py:597
  74.3 2.5 %finish.1 = (f32[16,8192]{1,0:T(8,128)}, f32[16,8192]{1,0:T(8,128)}, f32[2,2,8,8]{3,2,1,0:T(8,128)}) custom-call(f32[16,8192]{1,0:T(8,128)} %get-tuple-element.25.curl_hbm.curl_in, f32[16,8192]{1,0:T(8,128)} %get-tuple-element.26.mass_hbm.mass_in, f32[2,16,4096]{2,1,0:T(8,128)} %get-tuple-element.30.lows, ...), custom_call_target="tpu_custom_call", output_to_operand_aliasing={{0}: (0, {}), {1}: (1, {})} | custom-call | tf_op jit(solution)/shard_map/finish/pallas_call | solution.py:635

commit v8 on v7

--- a/solution.py
+++ b/solution.py
@@ -482,8 +482,9 @@
     def greet(device):
         pl.semaphore_signal(barrier, 1, device_id=device, device_id_type=pl.DeviceIdType.MESH)
 
-    for place, me in groups:
-        for k in range(1, GROUP):
+    far_first = sorted(range(1, GROUP), key=lambda k: -min(k, GROUP - k))
+    for place, me in reversed(groups):
+        for k in far_first:
             greet(place(lax.rem(me + k, GROUP)))
     greet(next_x)
     greet(last_x)
@@ -518,7 +519,7 @@
         )
 
     def others(me):
-        return [lax.rem(me + k, GROUP) for k in range(1, GROUP)]
+        return [lax.rem(me + k, GROUP) for k in far_first]
 
     def send_all(phase, source):
         me = groups[phase][1]

time: 76.6 us -> 73.6 us (0.961); the launches traced: 76.8 us -> 72.3 us
  Pallas kernels: 75.5 us -> 71 us
    pallas_call x1, Pallas kernels: 38.5 us -> 34 us  [exchange(): pl.pallas_call(exchange_kernel, out_shape=(shape((2, ROWS, 2 * face), f32...]
where the time goes in v8:
time: 73.6 us; the launch traced here: 72.3 us
  Pallas kernels  71 us (96%)
  between operations  1.3 us (2%)
    pallas_call x1, Pallas kernels, exchange(): pl.pallas_call(exchange_kernel, out_shape=(shape((2, ROWS, 2 * face), f32...  34 us
    pallas_call x1, Pallas kernels, part_images(): pl.pallas_call(part_kernel, out_shape=(shape((ROWS, owned), f32), shape((...  22.1 us
    pallas_call x1, Pallas kernels, begin(): pl.pallas_call(begin_kernel, out_shape=(high, high, shape((2, LANES), jnp...  12.4 us
    pallas_call x1, Pallas kernels, finish(): pl.pallas_call(finish_kernel, out_shape=tuple((shape(value.shape, jnp.flo...  2.46 us

profile of v8, /device:TPU:1, one launch (start us, length us, event | category | flops | bytes accessed | tf_op | source)
XLA Modules:
  0.0 72.3 jit_solution(18445423896620003735)
XLA Ops:
  1.3 12.4 %begin.1 = (f32[16,2048]{1,0:T(8,128)}, f32[16,2048]{1,0:T(8,128)}, f32[2,128]{1,0:T(2,128)}, s32[160,128]{1,0:T(8,128)}, bf16[384,640]{1,0:T(8,128)(2,1)}, /*index=5*/bf16[384,640]{1,0:T(8,128)(2,1)}) custom-call(s32[2]{0:T(128)} %fraction_ref.1, f32[16,8192]{1,0:T(8,128)} %bitcast.12, s32[20,1,1024]{2,1,0:T(1,128)} %bitcast.15, s32[16,128]{1,0:T(8,128)} %bitcast.16, ...), custom_call_target="tpu_custom_call" | custom-call | tf_op jit(solution)/shard_map/begin/pallas_call | solution.py:166
  13.7 22.1 %part_images.1 = (f32[16,8192]{1,0:T(8,128)}, f32[16,8192]{1,0:T(8,128)}, f32[32,2048]{1,0:T(8,128)}, f32[32,2048]{1,0:T(8,128)}, f32[8,128]{1,0:T(8,128)}) custom-call(s32[1,1]{1,0:T(1,128)S(6)} %copy.16.count_ref, s32[20480]{0:T(1024)} %bitcast.14, f32[16,8192]{1,0:T(8,128)} %bitcast.13, f32[16,2048]{1,0:T(8,128)} %get-tuple-element.20.high_x_hbm, ...), custom_call_target="tpu_custom_call" | custom-call | tf_op jit(solution)/shard_map/part_images/pallas_call | solution.py:409
  35.8 34.0 %exchange.1 = (f32[2,16,4096]{2,1,0:T(8,128)}, f32[2,2,8,8]{3,2,1,0:T(8,128)}) custom-call(f32[32,2048]{1,0:T(8,128)} %get-tuple-element.27.side_x_hbm, f32[32,2048]{1,0:T(8,128)} %get-tuple-element.28.side_y_hbm, f32[16,8192]{1,0:T(8,128)} %get-tuple-element.25.curl_hbm.curl_in, f32[16,8192]{1,0:T(8,128)} %get-tuple-element.26.mass_hbm.mass_in, ...), custom_call_target="tpu_custom_call" | custom-call | tf_op jit(solution)/shard_map/exchange/pallas_call | solution.py:598
  69.8 2.5 %finish.1 = (f32[16,8192]{1,0:T(8,128)}, f32[16,8192]{1,0:T(8,128)}, f32[2,2,8,8]{3,2,1,0:T(8,128)}) custom-call(f32[16,8192]{1,0:T(8,128)} %get-tuple-element.25.curl_hbm.curl_in, f32[16,8192]{1,0:T(8,128)} %get-tuple-element.26.mass_hbm.mass_in, f32[2,16,4096]{2,1,0:T(8,128)} %get-tuple-element.30.lows, ...), custom_call_target="tpu_custom_call", output_to_operand_aliasing={{0}: (0, {}), {1}: (1, {})} | custom-call | tf_op jit(solution)/shard_map/finish/pallas_call | solution.py:636
